TPU v7x, 256 devices: a whole 4x4x8 slice. The times are simulated.
256 devices in a mesh: prow: 16 (over x, y), pcol: 16 (over z, core).
Axes of the slice: x: 4, y: 4, z: 8, core: 2. Of those that a mesh axis runs over, the one named last changes fastest.
Arguments:
- diag_inverse: float32 [2, 1024, 1024], P(None, 'pcol', 'prow'), as said below
- coupling: float32 [1024, 1024], P('prow', 'pcol'), may hold values from -0.1875 to 0.1875
- rhs_top: float32 [2, 1024, 1024], P(None, 'prow'), may hold values from -6 to 6
- panel: float32 [65536, 2048], P('prow', 'pcol'), may hold values from -0.1875 to 0.1875
- rhs_rest: float32 [65536, 1024], P(('prow', 'pcol')), may hold values from -6 to 6
Outputs:
- adjoint_top: float32 [2, 1024, 1024], P(None, 'pcol')
- rhs_updated: float32 [65536, 1024], P(('prow', 'pcol'))
Inputs may be any that keep to these rules, and one draw needn't show every extreme that they name: Each of the two blocks of diag_inverse is lower triangular, with zeros above the diagonal.
All inputs are finite; a program needn't handle non-finite values.
Results may differ from a plain program's by a relative error of at most 0.000065.
Values sent between devices are 32-bit elements; how exact they have to be, the bound alone decides.
A program may use at most 64 MiB of HBM per device.

v0:
```python
import jax
import jax.numpy as jnp
from jax import lax
from jax.sharding import PartitionSpec as P

precise = lax.Precision.HIGHEST


def product(left_side, right_side):
    return jnp.dot(left_side, right_side, precision=precise, preferred_element_type=jnp.float32)


def body(diag_inverse, coupling, rhs_top, panel, rhs_rest):
    first_solution = lax.psum(product(diag_inverse[0], rhs_top[0]), "prow")
    carried = lax.psum(product(coupling, first_solution), "pcol")
    second_solution = lax.psum(product(diag_inverse[1], rhs_top[1] - carried), "prow")
    stacked = jnp.concatenate([first_solution, second_solution], axis=0)
    summed = lax.psum_scatter(product(panel, stacked), "pcol", scatter_dimension=0, tiled=True)
    adjoint_top = jnp.stack([first_solution, second_solution])
    return (adjoint_top, rhs_rest - summed)


def solution(mesh):
    in_specs = (
        P(None, "pcol", "prow"),
        P("prow", "pcol"),
        P(None, "prow", None),
        P("prow", "pcol"),
        P(("prow", "pcol"), None),
    )
    out_specs = (P(None, "pcol", None), P(("prow", "pcol"), None))
    return jax.shard_map(body, mesh=mesh, in_specs=in_specs, out_specs=out_specs, check_vma=False)
```

profile of v0, /device:TPU:1, one launch (start us, length us, event | category | flops | bytes accessed | tf_op | source)
XLA Modules:
  0.0 446.6 jit_solution(18211747163709749124)
XLA Ops:
  7.2 0.0 copy-start
  7.2 0.0 all-reduce.4.cloned.1.call-start
  7.2 2.2 fusion.3
  9.4 0.0 all-reduce.4.cloned.1.call-update
  9.4 0.0 all-reduce.6.cloned.1.call-start
  9.5 99.2 %all-reduce.4.cloned.1.call-done = f32[64,1024]{1,0:T(8,128)} async-done(((f32[64,1024]{1,0:T(8,128)}), f32[64,1024]{1,0:T(8,128)}) %all-reduce.4.cloned.1.call-update) | async-done | bytes 262160 | tf_op jit(solution)/shard_map/psum | solution.py:14
  108.7 2.0 convolution_bitcast_fusion.2
  110.7 0.0 all-reduce.6.cloned.1.call-update
  110.7 0.0 all-reduce.8.cloned.1.call-start
  110.8 110.0 %all-reduce.6.cloned.1.call-done = f32[64,1024]{1,0:T(8,128)} async-done(((f32[64,1024]{1,0:T(8,128)}), f32[64,1024]{1,0:T(8,128)}) %all-reduce.6.cloned.1.call-update) | async-done | bytes 262160 | tf_op jit(solution)/shard_map/psum | solution.py:15
  220.8 2.1 convolution_bitcast_fusion.1
  222.9 0.0 all-reduce.8.cloned.1.call-update
  222.9 0.0 reduce-scatter.2.cloned.1.call-start
  223.0 95.0 %all-reduce.8.cloned.1.call-done = f32[64,1024]{1,0:T(8,128)} async-done(((f32[64,1024]{1,0:T(8,128)}), f32[64,1024]{1,0:T(8,128)}) %all-reduce.8.cloned.1.call-update) | async-done | bytes 262160 | tf_op jit(solution)/shard_map/psum | solution.py:16
  317.9 0.0 copy-done
  317.9 17.0 %convolution_bitcast_fusion = f32[4096,1024]{0,1:T(8,128)} fusion(f32[4096,128]{1,0:T(8,128)S(1)} %copy-done, f32[64,1024]{1,0:T(8,128)} %all-reduce.8.cloned.1.call-done, f32[64,1024]{1,0:T(8,128)} %all-reduce.4.cloned.1.call-done), kind=kOutput, calls=%fused_computation | convolution fusion | flops 6442582016 | bytes 19398656 | tf_op jit(solution)/shard_map/dot_general | solution.py:10
  334.9 0.0 reduce-scatter.2.cloned.1.call-update
  334.9 0.0 copy-start.1
  335.0 1.6 copy.7
  336.6 0.0 copy-done.1
  336.6 1.8 pad_maximum_fusion
  338.4 96.9 %reduce-scatter.2.cloned.1.call-done = f32[256,1024]{0,1:T(8,128)} async-done(((f32[4096,1024]{0,1:T(8,128)}), f32[256,1024]{0,1:T(8,128)}) %reduce-scatter.2.cloned.1.call-update) | async-done | bytes 1048592 | tf_op jit(solution)/shard_map/reduce_scatter | solution.py:18
  435.3 2.3 sub.7
  437.6 2.5 copy.8
Async XLA Ops:
  7.2 310.8 %copy-start = (f32[4096,128]{1,0:T(8,128)S(1)}, f32[4096,128]{1,0:T(8,128)}, u32[]{:S(2)}) copy-start(f32[4096,128]{1,0:T(8,128)} %param.8) | copy-start | bytes 6291460
  7.2 101.5 %all-reduce.4.cloned.1.call-start = ((), (), s32[]{:S(2)}) async-start(), calls=%async_computation.1 | async-start | bytes 524288 | tf_op jit(solution)/shard_map/psum | solution.py:14
  9.4 211.3 %all-reduce.6.cloned.1.call-start = ((), (), s32[]{:S(2)}) async-start(), calls=%async_computation.2 | async-start | bytes 524288 | tf_op jit(solution)/shard_map/psum | solution.py:15
  110.7 207.2 %all-reduce.8.cloned.1.call-start = ((), (), s32[]{:S(2)}) async-start(), calls=%async_computation.3 | async-start | bytes 524288 | tf_op jit(solution)/shard_map/psum | solution.py:16
  222.9 212.4 %reduce-scatter.2.cloned.1.call-start = ((), (), s32[]{:S(2)}) async-start(), calls=%async_computation.4 | async-start | bytes 17825792 | tf_op jit(solution)/shard_map/reduce_scatter | solution.py:18
  334.9 1.6 copy-start.1
Sparse Core Ops, SparseCore 0:
  11.8 96.8 all-reduce.3
  111.7 109.0 all-reduce.5
  224.5 93.3 all-reduce.7
  335.1 100.1 reduce-scatter.1
where the time goes:
time: 447 us
  waiting for transfers between devices  401 us (90%)
  matrix products  23.3 us (5%)
  between operations  13.8 us (3%)
    psum x1, waiting for transfers between devices, body(): carried = lax.psum(product(coupling, first_solution), 'pcol')  110 us
    psum x1, waiting for transfers between devices, body(): first_solution = lax.psum(product(diag_inverse[0], rhs_top[0]), 'prow')  99.2 us
    reduce_scatter x1, waiting for transfers between devices, body(): lax.psum_scatter(product(panel, stacked), 'pcol', scatter_dimension=0, ti...  96.9 us
    psum x1, waiting for transfers between devices, body(): lax.psum(product(diag_inverse[1], rhs_top[1] - carried), 'prow')  95 us
    dot_general x4, matrix products, product(): jnp.dot(left_side, right_side, precision=precise, preferred_element_type=...  23.3 us
  transfers between devices with their start and end apart: 4, of which 4 were waited for; matrix products, arithmetic and copies ran while one was open for 1% of the time, Pallas kernels for 0%

commit v1 on v0

v1 whole, which is shorter than its diff:
```python
import jax
import jax.numpy as jnp
from jax import lax
from jax.experimental import pallas as pl
from jax.experimental.pallas import tpu as pltpu
from jax.sharding import PartitionSpec as P

MESH = pl.DeviceIdType.MESH
F32, BF16 = jnp.float32, jnp.bfloat16


def precise(a, b):
    return jnp.dot(a, b, precision=lax.Precision.HIGHEST, preferred_element_type=F32)


def coarse(a, b):
    return jnp.dot(a, b, preferred_element_type=F32)


def remote(src, dst, send, recv, device):
    return pltpu.make_async_remote_copy(
        src_ref=src, dst_ref=dst, send_sem=send, recv_sem=recv, device_id=device, device_id_type=MESH
    )


def kernel(
    d_ref, c_ref, b_ref, p_ref, rest_ref, adj_ref, out_ref,
    d_v, c_v, b_v, p_v, pr_v, o_v, adj_v,
    cz, dm, us, ur, v1, es, er, eg, ms, mr, gx, gs, xh, xl,
    ld, st, p_s, p_r, c_s, c_r, d_s, d_r, u_s, u_r, e_s, e_r, g_s, g_r, m_s, m_r, z_s, z_r, a_s, a_r, f_s, f_r, x_s, x_r,
):
    r, c = lax.axis_index("prow"), lax.axis_index("pcol")
    x, y, z, k = r // 4, r % 4, c // 2, c % 2
    h = r % 2
    mate, twin = r + 1 - 2 * h, c + 1 - 2 * k

    def row(d):
        return (r + d) % 16

    def col(d):
        return (c + d) % 16

    def at_z(d):
        return ((z + d) % 8) * 2 + k

    def loop(low, high, body):
        def step(i, carry):
            body(i)
            return carry

        lax.fori_loop(low, high, step, 0)

    loads = [
        pltpu.make_async_copy(src, dst, ld.at[i])
        for i, (src, dst) in enumerate([(d_ref, d_v), (c_ref, c_v), (b_ref, b_v), (p_ref, p_v), (rest_ref, o_v)])
    ]
    for load in loads:
        load.start()
    pltpu.make_async_copy(p_ref.at[c], pr_v.at[c], p_r.at[0]).start()

    barrier = pltpu.get_barrier_semaphore()

    def greet(d):
        pl.semaphore_signal(barrier, inc=1, device_id=(r, col(d)), device_id_type=MESH)
        pl.semaphore_signal(barrier, inc=1, device_id=(row(d), c), device_id_type=MESH)

    loop(1, 16, greet)
    pl.semaphore_signal(barrier, inc=1, device_id=(mate, twin), device_id_type=MESH)
    for load in loads[:3]:
        load.wait()
    cz[z] = jnp.concatenate([c_v[:32], c_v[32:]], axis=1)
    dm[k] = d_v[1]
    pl.semaphore_wait(barrier, 31)

    def c_copy(d):
        return remote(cz.at[z], cz.at[z], c_s.at[d], c_r.at[d], (r, at_z(d)))

    def c_here(d):
        there = (z + 8 - d) % 8
        return remote(cz.at[there], cz.at[there], c_s.at[d], c_r.at[d], (r, at_z(d)))

    loop(1, 8, lambda d: c_copy(d).start())
    d_copy = remote(dm.at[k], dm.at[k], d_s, d_r, (r, twin))
    d_copy.start()

    loads[3].wait()

    def p_copy(d):
        return remote(p_v.at[col(d)], pr_v.at[c], p_s.at[d], p_r.at[d], (r, col(d)))

    loop(1, 16, lambda d: p_copy(d).start())

    for j in range(2):
        u = precise(d_v[j], b_v[j])
        for i in range(16):
            us[i, 32 * j : 32 * j + 32] = u[32 * (i % 2) : 32 * (i % 2) + 32, 128 * (i // 2) : 128 * (i // 2) + 128]

    def u_copy(d):
        return remote(us.at[row(d)], ur.at[d], u_s.at[d], u_r.at[d], (row(d), c))

    loop(1, 16, lambda d: u_copy(d).start())

    remote(dm.at[1 - k], dm.at[1 - k], d_s, d_r, (r, twin)).wait_recv()
    loop(1, 8, lambda d: c_here(d).wait_recv())
    upper = jnp.concatenate([cz[i][:, :64] for i in range(8)], axis=1)
    lower = jnp.concatenate([cz[i][:, 64:] for i in range(8)], axis=1)
    e = precise(dm[...].reshape(128, 64), jnp.concatenate([upper, lower], axis=0))
    for i in range(16):
        es[i] = e[32 * (i // 4) : 32 * (i // 4) + 32, 128 * (i % 4) : 128 * (i % 4) + 128]

    def e_copy(d):
        return remote(es.at[row(d)], er.at[d], e_s.at[d], e_r.at[d], (row(d), c))

    loop(1, 16, lambda d: e_copy(d).start())

    loop(1, 16, lambda d: u_copy(d).wait_recv())
    ur[0] = us[r]
    total = ur[0]
    for d in range(1, 16):
        total += ur[d]
    gx[0, x, y, z] = total[:32]
    v1[...] = total[32:]

    def z_copy(j, d):
        return remote(gx.at[j, x, y, z], gx.at[j, x, y, z], z_s.at[j, d], z_r.at[j, d], (r, at_z(d)))

    def z_here(j, d):
        there = (z + 8 - d) % 8
        return remote(gx.at[j, x, y, there], gx.at[j, x, y, there], z_s.at[j, d], z_r.at[j, d], (r, at_z(d)))

    loop(1, 8, lambda d: z_copy(0, d).start())

    loop(1, 16, lambda d: e_copy(d).wait_recv())
    er[0] = es[r]
    total = er[0]
    for d in range(1, 16):
        total += er[d]
    eg[r] = total

    def g_copy(d):
        return remote(eg.at[r], eg.at[r], g_s.at[d], g_r.at[d], (row(d), c))

    def g_here(d):
        there = (r + 16 - d) % 16
        return remote(eg.at[there], eg.at[there], g_s.at[d], g_r.at[d], (row(d), c))

    loop(1, 16, lambda d: g_copy(d).start())

    near, far = pl.ds(0, 4), pl.ds(4, 4)

    def a_copy(j, d, there=False):
        xs, ys = ((x + 4 - d) % 4, (y + 4 - d) % 4) if there else (x, y)
        one, two = gx.at[j, xs, y, near], gx.at[j, x, ys, far]
        return (
            remote(one, one, a_s.at[j, 0, d], a_r.at[j, 0, d], (((x + d) % 4) * 4 + y, c)),
            remote(two, two, a_s.at[j, 1, d], a_r.at[j, 1, d], (x * 4 + (y + d) % 4, c)),
        )

    def f_copy(j, d, there=False):
        xs, ys = ((x + 4 - d) % 4, (y + 4 - d) % 4) if there else (x, y)
        one, two = gx.at[j, :, ys, near], gx.at[j, xs, :, far]
        return (
            remote(one, one, f_s.at[j, 0, d], f_r.at[j, 0, d], (x * 4 + (y + d) % 4, c)),
            remote(two, two, f_s.at[j, 1, d], f_r.at[j, 1, d], (((x + d) % 4) * 4 + y, c)),
        )

    def start(copies):
        for copy in copies:
            copy.start()

    def arrive(copies):
        for copy in copies:
            copy.wait_recv()

    def leave(copies):
        for copy in copies:
            copy.wait_send()

    loop(1, 8, lambda d: z_here(0, d).wait_recv())
    loop(1, 4, lambda d: start(a_copy(0, d)))

    loop(1, 16, lambda d: g_here(d).wait_recv())
    e = jnp.concatenate([jnp.concatenate([eg[4 * i + j] for j in range(4)], axis=1) for i in range(4)], axis=0)
    first = h == 0
    rows = []
    for i in range(8):
        block = gx[0, x, y, i]
        rows += [jnp.where(first, block, 0.0), jnp.where(first, 0.0, block)]
    ms[...] = precise(e, jnp.concatenate(rows, axis=0)).reshape(4, 32, 128)
    others = [(1 - k, h, (r, twin)), (k, 1 - h, (mate, c)), (1 - k, 1 - h, (mate, twin))]
    m_copies = [
        remote(ms.at[2 * kk + hh], mr.at[i], m_s.at[i], m_r.at[i], device) for i, (kk, hh, device) in enumerate(others)
    ]
    start(m_copies)
    loop(1, 4, lambda d: arrive(a_copy(0, d, True)))
    loop(1, 4, lambda d: start(f_copy(0, d)))
    arrive(m_copies)
    gx[1, x, y, z] = v1[...] - (ms[2 * k + h] + mr[0] + mr[1] + mr[2])
    loop(1, 8, lambda d: z_copy(1, d).start())
    loop(1, 8, lambda d: z_here(1, d).wait_recv())
    loop(1, 4, lambda d: start(a_copy(1, d)))
    loop(1, 4, lambda d: arrive(a_copy(1, d, True)))
    loop(1, 4, lambda d: start(f_copy(1, d)))

    def x_copy(j):
        return remote(gx.at[j], gs.at[j], x_s.at[j], x_r.at[j], (r, twin))

    def split(held, j, kk):
        def body(i):
            q = 2 * i + kk
            for n in range(16):
                value = held[j, n // 4, n % 4, i]
                high = value.astype(BF16)
                rows = slice(64 * j + 32 * (n % 2), 64 * j + 32 * (n % 2) + 32)
                lanes = slice(128 * (n // 2), 128 * (n // 2) + 128)
                xh[q, rows, lanes] = high
                xl[q, rows, lanes] = (value - high.astype(F32)).astype(BF16)

        loop(0, 8, body)

    for j in range(2):
        loop(1, 4, lambda d: arrive(f_copy(j, d, True)))
        x_copy(j).start()
        split(gx, j, k)
        for n in range(16):
            adj_v[j, 32 * (n % 2) : 32 * (n % 2) + 32, 128 * (n // 2) : 128 * (n // 2) + 128] = gx[j, n // 4, n % 4, z]
        x_copy(j).wait_recv()
        split(gs, j, 1 - k)
    adj_out = pltpu.make_async_copy(adj_v, adj_ref, st.at[0])
    adj_out.start()

    loads[4].wait()

    def update(i):
        there = (z + 8 + (2 * (i % 2) - 1) * ((i + 1) // 2)) % 8
        for kk in range(2):
            q = 2 * there + kk
            d = (c + 16 - q) % 16
            remote(p_v.at[q], pr_v.at[q], p_s.at[d], p_r.at[d], (r, col(1))).wait_recv()
        block = jnp.concatenate([pr_v[2 * there], pr_v[2 * there + 1]], axis=1)
        high = block.astype(BF16)
        low = (block - high.astype(F32)).astype(BF16)
        x_high = xh[pl.ds(2 * there, 2)].reshape(256, 1024)
        x_low = xl[pl.ds(2 * there, 2)].reshape(256, 1024)
        o_v[...] -= coarse(high, x_high) + (coarse(high, x_low) + coarse(low, x_high))

    loop(0, 8, update)
    out = pltpu.make_async_copy(o_v, out_ref, st.at[1])
    out.start()

    d_copy.wait_send()
    loop(1, 8, lambda d: c_copy(d).wait_send())
    for j in range(2):
        loop(1, 8, lambda d: z_copy(j, d).wait_send())
        loop(1, 4, lambda d: leave(a_copy(j, d)))
        loop(1, 4, lambda d: leave(f_copy(j, d)))
        x_copy(j).wait_send()

    def left(d):
        p_copy(d).wait_send()
        u_copy(d).wait_send()
        e_copy(d).wait_send()
        g_copy(d).wait_send()

    loop(1, 16, left)
    leave(m_copies)
    adj_out.wait()
    out.wait()


def body(diag_inverse, coupling, rhs_top, panel, rhs_rest):
    vmem, sem = pltpu.VMEM, pltpu.SemaphoreType.DMA
    scratch = [
        vmem((2, 64, 64), F32), vmem((64, 64), F32), vmem((2, 64, 1024), F32), vmem((16, 256, 128), F32),
        vmem((16, 256, 128), F32), vmem((256, 1024), F32), vmem((2, 64, 1024), F32),
        vmem((8, 32, 128), F32), vmem((2, 64, 64), F32), vmem((16, 64, 128), F32), vmem((16, 64, 128), F32),
        vmem((32, 128), F32), vmem((16, 32, 128), F32), vmem((16, 32, 128), F32), vmem((16, 32, 128), F32),
        vmem((4, 32, 128), F32), vmem((3, 32, 128), F32),
        vmem((2, 4, 4, 8, 32, 128), F32), vmem((2, 4, 4, 8, 32, 128), F32),
        vmem((16, 128, 1024), BF16), vmem((16, 128, 1024), BF16),
        sem((5,)), sem((2,)), sem((16,)), sem((16,)), sem((8,)), sem((8,)), sem, sem,
        sem((16,)), sem((16,)), sem((16,)), sem((16,)), sem((16,)), sem((16,)), sem((3,)), sem((3,)),
        sem((2, 8)), sem((2, 8)), sem((2, 2, 4)), sem((2, 2, 4)), sem((2, 2, 4)), sem((2, 2, 4)), sem((2,)), sem((2,)),
    ]
    return pl.pallas_call(
        kernel,
        out_shape=(jax.ShapeDtypeStruct((2, 64, 1024), F32), jax.ShapeDtypeStruct((256, 1024), F32)),
        in_specs=[pl.BlockSpec(memory_space=pl.ANY)] * 5,
        out_specs=[pl.BlockSpec(memory_space=pl.ANY)] * 2,
        scratch_shapes=scratch,
        compiler_params=pltpu.CompilerParams(collective_id=0, has_side_effects=True, vmem_limit_bytes=48 * 2**20),
        name="window",
    )(diag_inverse, coupling, rhs_top, panel.reshape(16, 256, 128), rhs_rest)


def solution(mesh):
    in_specs = (
        P(None, "pcol", "prow"),
        P("prow", "pcol"),
        P(None, "prow", None),
        P("prow", "pcol"),
        P(("prow", "pcol"), None),
    )
    out_specs = (P(None, "pcol", None), P(("prow", "pcol"), None))
    return jax.shard_map(body, mesh=mesh, in_specs=in_specs, out_specs=out_specs, check_vma=False)
```

time: 447 us -> 117 us (0.26)
  waiting for transfers between devices: 401 us -> 0 us
  Pallas kernels: 0 us -> 109 us
  matrix products: 23.3 us -> 0 us
  between operations: 13.8 us -> 0.65 us
    psum x3 -> x0, waiting for transfers between devices: 304 us -> none  [the longest x1 110 us: body(): carried = lax.psum(product(coupling, first_solution), 'pcol')]
    pallas_call x0 -> x1, Pallas kernels: none -> 109 us  [body(): pl.pallas_call(kernel, out_shape=(jax.ShapeDtypeStruct((2, 64, 1024), F32...]
    reduce_scatter x1 -> x0, waiting for transfers between devices: 96.9 us -> none  [body(): lax.psum_scatter(product(panel, stacked), 'pcol', scatter_dimension=0, ti...]
    dot_general x4 -> x0, matrix products: 23.3 us -> none  [product(): jnp.dot(left_side, right_side, precision=precise, preferred_element_type=...]
  transfers between devices with their start and end apart: 4 -> 0, of which waited for: 4 -> 0; matrix products, arithmetic and copies ran while one was open for 1% -> 0% of each run, Pallas kernels for 0% -> 0%
where the time goes in v1:
time: 117 us
  Pallas kernels  109 us (93%)
  local copies, waits for them, and re-layouts  7.21 us (6%)
    pallas_call x1, Pallas kernels, body(): pl.pallas_call(kernel, out_shape=(jax.ShapeDtypeStruct((2, 64, 1024), F32...  109 us
    unnamed x12, local copies, waits for them, and re-layouts  7.21 us

profile of v1, /device:TPU:1, one launch (start us, length us, event | category | flops | bytes accessed | tf_op | source)
XLA Modules:
  0.0 117.1 jit_solution(16953349693379550893)
XLA Ops:
  0.6 0.0 copy-start
  0.6 1.6 %copy-done = f32[4096,128]{1,0:T(8,128)S(1)} copy-done((f32[4096,128]{1,0:T(8,128)S(1)}, f32[4096,128]{1,0:T(8,128)}, u32[]{:S(2)}) %copy-start) | copy-done | bytes 2097176
  2.2 0.0 copy-start.1
  2.2 1.2 %copy-done.1 = f32[256,1024]{1,0:T(8,128)S(1)} copy-done((f32[256,1024]{1,0:T(8,128)S(1)}, f32[256,1024]{1,0:T(8,128)}, u32[]{:S(2)}) %copy-start.1) | copy-done | bytes 1048600
  3.4 0.0 copy-start.2
  3.5 1.0 copy-done.2
  4.5 0.0 copy-start.3
  4.5 0.8 copy-done.3
  5.3 0.0 copy-start.4
  5.3 0.8 copy-done.4
  6.1 109.2 %window.1 = (f32[2,64,1024]{2,1,0:T(8,128)S(1)}, f32[256,1024]{1,0:T(8,128)S(1)}) custom-call(f32[2,64,64]{2,1,0:T(8,128)S(1)} %copy-done.3, f32[64,64]{1,0:T(8,128)S(1)} %copy-done.4, f32[2,64,1024]{2,1,0:T(8,128)S(1)} %copy-done.2, f32[16,256,128]{2,1,0:T(8,128)S(1)} %bitcast.1, f32[256,1024]{1,0:T(8,128)S(1)} %copy-done.1), custom_call_target="tpu_custom_call" | custom-call | tf_op jit(solution)/shard_map/window/pallas_call | solution.py:285
  115.3 0.8 copy.9
  116.1 1.0 copy.10
Async XLA Ops:
  0.6 1.6 %copy-start = (f32[4096,128]{1,0:T(8,128)S(1)}, f32[4096,128]{1,0:T(8,128)}, u32[]{:S(2)}) copy-start(f32[4096,128]{1,0:T(8,128)} %param.8) | copy-start | bytes 6291460
  2.2 1.2 %copy-start.1 = (f32[256,1024]{1,0:T(8,128)S(1)}, f32[256,1024]{1,0:T(8,128)}, u32[]{:S(2)}) copy-start(f32[256,1024]{1,0:T(8,128)} %rest_ref.1) | copy-start | bytes 3145732
  3.4 1.0 copy-start.2
  4.5 0.8 copy-start.3
  5.3 0.8 copy-start.4

commit v2 on v0

v2 whole, which is shorter than its diff:
```python
import jax
import jax.numpy as jnp
from jax import lax
from jax.experimental import pallas as pl
from jax.experimental.pallas import tpu as pltpu
from jax.sharding import PartitionSpec as P

MESH = pl.DeviceIdType.MESH
F32, BF16 = jnp.float32, jnp.bfloat16


def precise(a, b):
    return jnp.dot(a, b, precision=lax.Precision.HIGHEST, preferred_element_type=F32)


def coarse(a, b):
    return jnp.dot(a, b, preferred_element_type=F32)


def remote(src, dst, send, recv, device):
    return pltpu.make_async_remote_copy(
        src_ref=src, dst_ref=dst, send_sem=send, recv_sem=recv, device_id=device, device_id_type=MESH
    )


def loop(low, high, body):
    def step(i, carry):
        body(i)
        return carry

    lax.fori_loop(low, high, step, 0)


def kernel(
    d_ref, c_ref, b_ref, p_ref, rest_ref, adj_ref, out_ref,
    d_v, c_v, b_v, p_v, pr_v, o_v, adj_v, d_t, c_t,
    cz, us, ur, v1, es, er, eg, ms, mr, gx, xh, xl,
    ld, st, p_s, p_r, h_s, h_r, d_s, d_r, c_s, c_r, u_s, u_r, e_s, e_r, g_s, g_r, m_s, m_r, z_s, z_r, n_s, n_r, f_s, f_r, x_s, x_r,
):
    r, c = lax.axis_index("prow"), lax.axis_index("pcol")
    x, y, z, k = r // 4, r % 4, c // 2, c % 2
    h = r % 2
    mate, twin = r + 1 - 2 * h, c + 1 - 2 * k
    pump, chain = k == 0, k == 1

    def row(d):
        return (r + d) % 16

    def at_z(d):
        return (z + d) % 8

    def back_z(d):
        return (z + 8 - d) % 8

    loads = [
        pltpu.make_async_copy(src, dst, ld.at[i])
        for i, (src, dst) in enumerate(
            [(d_ref, d_v), (c_ref, c_v), (b_ref, b_v), (p_ref, p_v.at[:, 0]), (rest_ref, o_v), (p_ref.at[c], pr_v.at[z, k])]
        )
    ]
    for load in loads:
        load.start()

    barrier = pltpu.get_barrier_semaphore()

    def greet(*device):
        pl.semaphore_signal(barrier, inc=1, device_id=device, device_id_type=MESH)

    greet(r, twin)
    loop(2, 16, lambda d: greet(r, (2 * z + d) % 16))

    @pl.when(chain)
    def _():
        loop(1, 16, lambda d: greet(row(d), c))

    for load in loads[:4]:
        load.wait()

    @pl.when(pump)
    def _():
        pl.semaphore_wait(barrier, 15)

    @pl.when(chain)
    def _():
        pl.semaphore_wait(barrier, 30)

    def away(i):
        return (4 + (2 * (i % 2) - 1) * ((i + 1) // 2)) % 8

    def p_copy(kk, i):
        q = 2 * at_z(away(i // 2)) + i % 2
        return remote(p_v.at[q, kk], pr_v.at[z, kk], p_s.at[kk, i], p_r.at[kk, i // 2], (r, q))

    def p_here(kk, i):
        there = back_z(away(i))
        return remote(pr_v.at[there, kk], pr_v.at[there, kk], p_s.at[kk, i], p_r.at[kk, i], (r, twin))

    def hand(i):
        q = 2 * at_z(away(i // 2)) + i % 2
        return remote(p_v.at[q, 0], p_v.at[q, 1], h_s.at[i], h_r.at[i], (r, twin))

    def swap():
        return remote(p_v.at[twin, 0], pr_v.at[z, k], h_s.at[14], h_r.at[14], (r, twin))

    def swap_here():
        return remote(p_v.at[twin, 0], pr_v.at[z, 1 - k], h_s.at[14], h_r.at[14], (r, twin))

    d_copy = remote(d_v, d_t, d_s.at[0], d_r.at[0], (r, twin))
    t_copy = remote(c_v, c_t, d_s.at[1], d_r.at[1], (r, twin))

    def c_copy(d):
        return remote(cz.at[z], cz.at[z], c_s.at[d], c_r.at[d], (r, 2 * at_z(d) + k))

    def c_here(d):
        return remote(cz.at[back_z(d)], cz.at[back_z(d)], c_s.at[d], c_r.at[d], (r, c))

    def u_copy(d):
        return remote(us.at[row(d)], ur.at[d], u_s.at[d], u_r.at[d], (row(d), c))

    def e_copy(d):
        return remote(es.at[row(d)], er.at[d], e_s.at[d], e_r.at[d], (row(d), c))

    def g_copy(d):
        return remote(eg.at[r], eg.at[r], g_s.at[d], g_r.at[d], (row(d), c))

    def g_here(d):
        return remote(eg.at[row(16 - d)], eg.at[row(16 - d)], g_s.at[d], g_r.at[d], (row(d), c))

    def z_copy(j, d):
        return remote(gx.at[j, x, y, z], gx.at[j, x, y, z], z_s.at[j, d], z_r.at[j, d], (r, 2 * at_z(d) + k))

    def z_here(j, d):
        block = gx.at[j, x, y, back_z(d)]
        return remote(block, block, z_s.at[j, d], z_r.at[j, d], (r, c))

    m_copy = remote(ms.at[1 - h], mr, m_s, m_r, (mate, c))

    near, far = pl.ds(0, 4), pl.ds(4, 4)

    def along(axis, d):
        return (((x + d) % 4) * 4 + y, c) if axis == 0 else (x * 4 + (y + d) % 4, c)

    def n_copy(j, axis, d):
        return remote(gx.at[j, x, y], gx.at[j, x, y], n_s.at[j, axis, d], n_r.at[j, axis, d], along(axis, d))

    def n_here(j, axis, d):
        block = gx.at[j, (x + 4 - d) % 4, y] if axis == 0 else gx.at[j, x, (y + 4 - d) % 4]
        return remote(block, block, n_s.at[j, axis, d], n_r.at[j, axis, d], along(axis, d))

    def f_copy(j, axis, e, d):
        block = gx.at[j, (x + 4 - e) % 4, y, near] if axis == 0 else gx.at[j, x, (y + 4 - e) % 4, far]
        return remote(block, block, f_s.at[j, axis, e, d], f_r.at[j, axis, e, d], along(1 - axis, d))

    def f_here(j, axis, e, d):
        if axis == 0:
            block = gx.at[j, (x + 4 - e) % 4, (y + 4 - d) % 4, near]
        else:
            block = gx.at[j, (x + 4 - d) % 4, (y + 4 - e) % 4, far]
        return remote(block, block, f_s.at[j, axis, e, d], f_r.at[j, axis, e, d], (r, twin))

    def x_copy(j, e, d):
        block = gx.at[j, (x + 4 - e) % 4, (y + 4 - d) % 4]
        return remote(block, block, x_s.at[j, e, d], x_r.at[j, e, d], (r, twin))

    def split(j, e, d):
        xx, yy = (x + 4 - e) % 4, (y + 4 - d) % 4
        p, hh = 2 * xx + yy // 2, yy % 2

        def body(i):
            value = gx[j, xx, yy, i]
            high = value.astype(BF16)
            xh[p, i, hh, j] = high
            xl[p, i, hh, j] = (value - high.astype(F32)).astype(BF16)

        loop(0, 8, body)

    def axes(body):
        for axis in range(2):
            loop(1, 4, lambda d: body(axis, d))

    @pl.when(pump)
    def _():
        d_copy.start()
        t_copy.start()
        swap().start()
        loop(0, 14, lambda i: p_copy(0, i).start())

        def relay(i):
            hand(i).wait_recv()
            p_copy(1, i).start()

        loop(0, 14, relay)
        for j in range(2):

            def take(i):
                x_copy(j, i // 4, i % 4).wait_recv()
                split(j, i // 4, i % 4)

            loop(0, 16, take)

    @pl.when(chain)
    def _():
        t_copy.wait_recv()
        cz[z] = jnp.concatenate([c_t[...], c_v[...]], axis=1)
        loop(1, 8, lambda d: c_copy(d).start())

        d_copy.wait_recv()
        for j in range(2):
            for i, part in enumerate((d_t, d_v)):
                u = precise(part[j], b_v[j])
                for n in range(8):
                    us[2 * n + i, j] = u[:, 128 * n : 128 * n + 128]
        loop(1, 16, lambda d: u_copy(d).start())
        swap().start()
        loop(0, 14, lambda i: hand(i).start())

        loop(1, 8, lambda d: c_here(d).wait_recv())
        both = jnp.concatenate([d_t[1], d_v[1]], axis=0)
        for n in range(8):
            e = precise(both, cz[n])
            es[n] = e[:64]
            es[8 + n] = e[64:]
        loop(1, 16, lambda d: e_copy(d).start())

        loop(1, 16, lambda d: u_copy(d).wait_recv())
        ur[0] = us[r]
        gx[0, x, y, z] = sum(ur[d, 0] for d in range(16))
        loop(1, 8, lambda d: z_copy(0, d).start())
        v1[...] = sum(ur[d, 1] for d in range(16))

        loop(1, 16, lambda d: e_copy(d).wait_recv())
        er[0] = es[r]
        eg[r] = sum(er[d] for d in range(16))
        loop(1, 16, lambda d: g_copy(d).start())

        loop(1, 8, lambda d: z_here(0, d).wait_recv())
        axes(lambda axis, d: n_copy(0, axis, d).start())

        loop(1, 16, lambda d: g_here(d).wait_recv())
        first = h == 0
        wide = []
        for i in range(8):
            block = gx[0, x, y, i]
            wide += [jnp.where(first, block, 0.0), jnp.where(first, 0.0, block)]
        wide = jnp.concatenate(wide, axis=0)
        for i in range(2):
            ms[i] = precise(jnp.concatenate([eg[8 * i + n] for n in range(8)], axis=1), wide)
        m_copy.start()
        m_copy.wait_recv()
        gx[1, x, y, z] = v1[...] - (ms[h] + mr[...])
        loop(1, 8, lambda d: z_copy(1, d).start())

        def forward(j):
            def body(axis, e):
                n_here(j, axis, e).wait_recv()
                loop(1, 4, lambda d: f_copy(j, axis, e, d).start())

            axes(body)

        def cross(j):
            def body(i):
                e, d = i // 4, i % 4

                @pl.when((e > 0) & (d > 0))
                def _():
                    f_here(j, 0, e, d).wait_recv()
                    f_here(j, 1, d, e).wait_recv()

                x_copy(j, e, d).start()
                split(j, e, d)

            loop(0, 16, body)

        forward(0)
        loop(1, 8, lambda d: z_here(1, d).wait_recv())
        axes(lambda axis, d: n_copy(1, axis, d).start())
        cross(0)
        forward(1)
        cross(1)

    for n in range(8):
        for j in range(2):
            adj_v[j, :, 128 * n : 128 * n + 128] = gx[j, n // 2, 2 * (n % 2) + k, z]
    adj_out = pltpu.make_async_copy(adj_v, adj_ref, st.at[0])
    adj_out.start()

    loads[4].wait()
    loads[5].wait()
    swap_here().wait_recv()

    def update(there):
        block = jnp.concatenate([pr_v[there, 0], pr_v[there, 1]], axis=1)
        high = block.astype(BF16)
        low = (block - high.astype(F32)).astype(BF16)
        x_high = jnp.concatenate([xh[n, there].reshape(256, 128) for n in range(8)], axis=1)
        x_low = jnp.concatenate([xl[n, there].reshape(256, 128) for n in range(8)], axis=1)
        o_v[...] -= coarse(high, x_high) + (coarse(high, x_low) + coarse(low, x_high))

    def step(i):
        @pl.when(i > 0)
        def _():
            p_here(0, i - 1).wait_recv()
            p_here(1, i - 1).wait_recv()

        update(jnp.where(i == 0, z, back_z(away(i - 1))))

    loop(0, 8, step)
    out = pltpu.make_async_copy(o_v, out_ref, st.at[1])
    out.start()

    swap().wait_send()

    @pl.when(pump)
    def _():
        d_copy.wait_send()
        t_copy.wait_send()

        def left(i):
            p_copy(0, i).wait_send()
            p_copy(1, i).wait_send()

        loop(0, 14, left)

    @pl.when(chain)
    def _():
        loop(0, 14, lambda i: hand(i).wait_send())
        loop(1, 8, lambda d: c_copy(d).wait_send())

        def left(d):
            u_copy(d).wait_send()
            e_copy(d).wait_send()
            g_copy(d).wait_send()

        loop(1, 16, left)
        m_copy.wait_send()
        for j in range(2):
            loop(1, 8, lambda d: z_copy(j, d).wait_send())
            loop(0, 16, lambda i: x_copy(j, i // 4, i % 4).wait_send())

            def left(axis, e):
                n_copy(j, axis, e).wait_send()
                loop(1, 4, lambda d: f_copy(j, axis, e, d).wait_send())

            axes(left)

    adj_out.wait()
    out.wait()


def body(diag_inverse, coupling, rhs_top, panel, rhs_rest):
    vmem, sem = pltpu.VMEM, pltpu.SemaphoreType.DMA
    scratch = [
        vmem((2, 64, 64), F32), vmem((64, 64), F32), vmem((2, 64, 1024), F32), vmem((16, 2, 256, 128), F32),
        vmem((8, 2, 256, 128), F32), vmem((256, 1024), F32), vmem((2, 64, 1024), F32), vmem((2, 64, 64), F32), vmem((64, 64), F32),
        vmem((8, 64, 128), F32), vmem((16, 2, 64, 128), F32), vmem((16, 2, 64, 128), F32), vmem((64, 128), F32),
        vmem((16, 64, 128), F32), vmem((16, 64, 128), F32), vmem((16, 64, 128), F32), vmem((2, 64, 128), F32), vmem((64, 128), F32),
        vmem((2, 4, 4, 8, 64, 128), F32), vmem((8, 8, 2, 2, 64, 128), BF16), vmem((8, 8, 2, 2, 64, 128), BF16),
        sem((6,)), sem((2,)), sem((2, 14)), sem((2, 7)), sem((15,)), sem((15,)), sem((2,)), sem((2,)), sem((8,)), sem((8,)),
        sem((16,)), sem((16,)), sem((16,)), sem((16,)), sem((16,)), sem((16,)), sem, sem, sem((2, 8)), sem((2, 8)),
        sem((2, 2, 4)), sem((2, 2, 4)), sem((2, 2, 4, 4)), sem((2, 2, 4, 4)), sem((2, 4, 4)), sem((2, 4, 4)),
    ]
    return pl.pallas_call(
        kernel,
        out_shape=(jax.ShapeDtypeStruct((2, 64, 1024), F32), jax.ShapeDtypeStruct((256, 1024), F32)),
        in_specs=[pl.BlockSpec(memory_space=pl.ANY)] * 5,
        out_specs=[pl.BlockSpec(memory_space=pl.ANY)] * 2,
        scratch_shapes=scratch,
        compiler_params=pltpu.CompilerParams(collective_id=0, has_side_effects=True, vmem_limit_bytes=60 * 2**20),
        name="window",
    )(diag_inverse, coupling, rhs_top, panel.reshape(16, 256, 128), rhs_rest)


def solution(mesh):
    in_specs = (
        P(None, "pcol", "prow"),
        P("prow", "pcol"),
        P(None, "prow", None),
        P("prow", "pcol"),
        P(("prow", "pcol"), None),
    )
    out_specs = (P(None, "pcol", None), P(("prow", "pcol"), None))
    return jax.shard_map(body, mesh=mesh, in_specs=in_specs, out_specs=out_specs, check_vma=False)
```

time: 447 us -> 94.2 us (0.21)
  waiting for transfers between devices: 401 us -> 0 us
  Pallas kernels: 0 us -> 88.2 us
  matrix products: 23.3 us -> 0 us
  between operations: 13.8 us -> 0.64 us
    psum x3 -> x0, waiting for transfers between devices: 304 us -> none  [the longest x1 110 us: body(): carried = lax.psum(product(coupling, first_solution), 'pcol')]
    reduce_scatter x1 -> x0, waiting for transfers between devices: 96.9 us -> none  [body(): lax.psum_scatter(product(panel, stacked), 'pcol', scatter_dimension=0, ti...]
    pallas_call x0 -> x1, Pallas kernels: none -> 88.2 us  [body(): pl.pallas_call(kernel, out_shape=(jax.ShapeDtypeStruct((2, 64, 1024), F32...]
    dot_general x4 -> x0, matrix products: 23.3 us -> none  [product(): jnp.dot(left_side, right_side, precision=precise, preferred_element_type=...]
  transfers between devices with their start and end apart: 4 -> 0, of which waited for: 4 -> 0; matrix products, arithmetic and copies ran while one was open for 1% -> 0% of each run, Pallas kernels for 0% -> 0%
where the time goes in v2:
time: 94.2 us; the launch traced here: 93 us
  Pallas kernels  88.2 us (94%)
  local copies, waits for them, and re-layouts  4.19 us (4%)
    pallas_call x1, Pallas kernels, body(): pl.pallas_call(kernel, out_shape=(jax.ShapeDtypeStruct((2, 64, 1024), F32...  88.2 us
    unnamed x2, local copies, waits for them, and re-layouts  4.19 us

profile of v2, /device:TPU:1, one launch (start us, length us, event | category | flops | bytes accessed | tf_op | source)
XLA Modules:
  0.0 93.0 jit_solution(3960132795951145655)
XLA Ops:
  0.6 88.2 %window.1 = (f32[2,64,1024]{2,1,0:T(8,128)}, f32[256,1024]{1,0:T(8,128)}) custom-call(f32[2,64,64]{2,1,0:T(8,128)} %d_ref.1, f32[64,64]{1,0:T(8,128)} %c_ref.1, f32[2,64,1024]{2,1,0:T(8,128)} %b_ref.1, f32[16,256,128]{2,1,0:T(8,128)} %bitcast.1, f32[256,1024]{1,0:T(8,128)} %rest_ref.1), custom_call_target="tpu_custom_call" | custom-call | tf_op jit(solution)/shard_map/window/pallas_call | solution.py:362
  88.8 1.9 %copy.9 = f32[2,64,1024]{2,1,0:T(8,128)} copy(f32[2,64,1024]{2,1,0:T(8,128)} %get-tuple-element.4) | data formatting | bytes 1048576
  90.7 2.3 %copy.10 = f32[256,1024]{1,0:T(8,128)} copy(f32[256,1024]{1,0:T(8,128)} %get-tuple-element.5) | data formatting | bytes 2097152

commit v3 on v2

v3 whole, which is shorter than its diff:
```python
import jax
import jax.numpy as jnp
from jax import lax
from jax.experimental import pallas as pl
from jax.experimental.pallas import tpu as pltpu
from jax.sharding import PartitionSpec as P

MESH = pl.DeviceIdType.MESH
F32, BF16 = jnp.float32, jnp.bfloat16


def precise(a, b):
    return jnp.dot(a, b, precision=lax.Precision.HIGHEST, preferred_element_type=F32)


def coarse(a, b):
    return jnp.dot(a, b, preferred_element_type=F32)


def remote(src, dst, send, recv, device):
    return pltpu.make_async_remote_copy(
        src_ref=src, dst_ref=dst, send_sem=send, recv_sem=recv, device_id=device, device_id_type=MESH
    )


def loop(low, high, body):
    def step(i, carry):
        body(i)
        return carry

    lax.fori_loop(low, high, step, 0)


def kernel(
    d_ref, c_ref, b_ref, p_ref, rest_ref, adj_ref, out_ref,
    d_v, c_v, b_v, p_v, pr_v, o_v, adj_v, d_t,
    cz, us, ur, es, er, eg, gx, xh, xl,
    ld, st, p_s, p_r, h_s, h_r, d_s, d_r, c_s, c_r, u_s, u_r, e_s, e_r, g_s, g_r, z_s, z_r, n_s, n_r, o_s, o_r, f_s, f_r, x_s, x_r,
):
    r, c = lax.axis_index("prow"), lax.axis_index("pcol")
    x, y, z, k = r // 4, r % 4, c // 2, c % 2
    h = r % 2
    twin = c + 1 - 2 * k
    pump, chain = k == 0, k == 1

    def row(d):
        return (r + d) % 16

    def at_z(d):
        return (z + d) % 8

    def back_z(d):
        return (z + 8 - d) % 8

    loads = [
        pltpu.make_async_copy(src, dst, ld.at[i])
        for i, (src, dst) in enumerate(
            [(d_ref, d_v), (c_ref, c_v), (b_ref, b_v), (p_ref, p_v.at[:, 0]), (rest_ref, o_v), (p_ref.at[c], pr_v.at[z, k])]
        )
    ]
    for load in loads:
        load.start()

    barrier = pltpu.get_barrier_semaphore()

    def greet(*device):
        pl.semaphore_signal(barrier, inc=1, device_id=device, device_id_type=MESH)

    greet(r, twin)
    loop(2, 16, lambda d: greet(r, (2 * z + d) % 16))

    loop(1, 16, lambda d: greet(row(d), c))

    @pl.when(chain & (h == 0))
    def _():
        loop(1, 16, lambda d: greet(row(d), twin))

    @pl.when(chain & (h == 1))
    def _():
        loop(1, 8, lambda d: greet(row(2 * d), twin))

    for load in loads[:3]:
        load.wait()
    for j in range(2):
        u = precise(d_v[j], b_v[j])
        for n in range(8):
            us[j, n] = u[:, 128 * n : 128 * n + 128]
    cz[z, k] = jnp.concatenate([c_v[:32], c_v[32:]], axis=1)

    @pl.when(chain & (h == 1))
    def _():
        for j in range(2):
            ur[j, r] = us[j, r // 2]

    loads[3].wait()

    @pl.when(pump)
    def _():
        pl.semaphore_wait(barrier, 37 + 8 * h)

    @pl.when(chain)
    def _():
        pl.semaphore_wait(barrier, 30)

    def away(i):
        return (4 + (2 * (i % 2) - 1) * ((i + 1) // 2)) % 8

    def p_copy(kk, i):
        q = 2 * at_z(away(i // 2)) + i % 2
        return remote(p_v.at[q, kk], pr_v.at[z, kk], p_s.at[kk, i], p_r.at[kk, i // 2], (r, q))

    def p_here(kk, i):
        there = back_z(away(i))
        return remote(pr_v.at[there, kk], pr_v.at[there, kk], p_s.at[kk, i], p_r.at[kk, i], (r, twin))

    def hand(i):
        q = 2 * at_z(away(i // 2)) + i % 2
        return remote(p_v.at[q, 0], p_v.at[q, 1], h_s.at[i], h_r.at[i], (r, twin))

    def swap():
        return remote(p_v.at[twin, 0], pr_v.at[z, k], h_s.at[14], h_r.at[14], (r, twin))

    def swap_here():
        return remote(p_v.at[twin, 0], pr_v.at[z, 1 - k], h_s.at[14], h_r.at[14], (r, twin))

    d_copy = remote(d_v.at[1], d_t, d_s, d_r, (r, twin))

    def c_copy(d):
        return remote(cz.at[z, k], cz.at[z, k], c_s.at[d], c_r.at[k, d], (r, 2 * at_z(d)))

    def c_here(kk, d):
        block = cz.at[back_z(d), kk]
        return remote(block, block, c_s.at[d], c_r.at[kk, d], (r, twin))

    def u_copy(j, n):
        return remote(us.at[j, n], ur.at[j, r], u_s.at[j, n], u_r.at[j, r], (2 * n + k, 2 * z + 1))

    def u_here(j, i):
        return remote(us.at[j, 0], ur.at[j, i], u_s.at[j, 0], u_r.at[j, i], (r, twin))

    def unless_own(n, body):
        @pl.when(pump | (2 * n + 1 != r))
        def _():
            body()

    def u_send(j):
        loop(0, 8, lambda n: unless_own(n, lambda: u_copy(j, n).start()))

    def u_sent(j):
        loop(0, 8, lambda n: unless_own(n, lambda: u_copy(j, n).wait_send()))

    def u_arrive(j):
        def body(i):
            @pl.when((h == 0) | (i != r))
            def _():
                u_here(j, i).wait_recv()

        loop(0, 16, body)

    def e_copy(d):
        return remote(es.at[row(d)], er.at[d], e_s.at[d], e_r.at[d], (row(d), c))

    def g_copy(d):
        return remote(eg.at[r // 2], eg.at[r // 2], g_s.at[d], g_r.at[d], (row(2 * d), 2 * z + 1))

    def g_here(d):
        block = eg.at[row(16 - 2 * d) // 2]
        return remote(block, block, g_s.at[d], g_r.at[d], (r, twin))

    def z_copy(j, d):
        block = gx.at[j, x, y, z // 2, z % 2]
        return remote(block, block, z_s.at[j, d], z_r.at[j, d], (r, 2 * at_z(d) + k))

    def z_here(j, d):
        block = gx.at[j, x, y, back_z(d) // 2, back_z(d) % 2]
        return remote(block, block, z_s.at[j, d], z_r.at[j, d], (r, c))

    def along(axis, d):
        return (((x + d) % 4) * 4 + y, c) if axis == 0 else (x * 4 + (y + d) % 4, c)

    def n_copy(j, axis, d, i, a, on):
        block = gx.at[j, x, y, i, a]
        if on:
            return remote(block, block, n_s.at[j, axis, d, i], n_r.at[j, axis, d, i], along(axis, d))
        return remote(block, block, o_s.at[j, axis, d], o_r.at[j, axis, d], along(axis, d))

    def n_here(j, a, d, i):
        block = gx.at[j, (x + 4 - (1 - a) * d) % 4, (y + 4 - a * d) % 4, i, a]
        return remote(block, block, n_s.at[j, a, d, i], n_r.at[j, a, d, i], (r, twin))

    def o_all(j, axis, d, here):
        xx, yy = x, y
        if here:
            xx, yy = ((x + 4 - d) % 4, y) if axis == 0 else (x, (y + 4 - d) % 4)
        block = gx.at[j, xx, yy, :, 1 - axis]
        return remote(block, block, o_s.at[j, axis, d], o_r.at[j, axis, d], (r, twin))

    def f_copy(j, a, e, d, i):
        block = gx.at[j, (x + 4 - (1 - a) * e) % 4, (y + 4 - a * e) % 4, i, a]
        to = ((x + a * d) % 4) * 4 + (y + (1 - a) * d) % 4
        return remote(block, block, f_s.at[j, a, e, d], f_r.at[j, a, e, d], (to, c))

    def f_all(j, a, e, d):
        block = gx.at[j, (x + 4 - (1 - a) * e - a * d) % 4, (y + 4 - a * e - (1 - a) * d) % 4, :, a]
        return remote(block, block, f_s.at[j, a, e, d], f_r.at[j, a, e, d], (r, twin))

    def x_copy(j, e, d):
        block = gx.at[j, (x + 4 - e) % 4, (y + 4 - d) % 4]
        return remote(block, block, x_s.at[j, e, d], x_r.at[j, e, d], (r, twin))

    def split(j, e, d):
        xx, yy = (x + 4 - e) % 4, (y + 4 - d) % 4
        p, hh = 2 * xx + yy // 2, yy % 2

        def body(i):
            value = gx[j, xx, yy, i // 2, i % 2]
            high = value.astype(BF16)
            xh[p, i, hh, j] = high
            xl[p, i, hh, j] = (value - high.astype(F32)).astype(BF16)

        loop(0, 8, body)

    def side(i):
        return ((2 * (i % 2) - 1) * ((i + 1) // 2) + 8) % 8

    def spread(j):
        def body(i):
            @pl.when(i > 0)
            def _():
                z_here(j, side(i)).wait_recv()

            piece = back_z(side(i))
            for a in range(2):

                @pl.when(piece % 2 == a)
                def _():
                    for axis in (a, 1 - a):
                        for d in (1, 3, 2):
                            n_copy(j, axis, d, piece // 2, a, axis == a).start()

        loop(0, 8, body)

    def forward(j):
        def body(i):
            piece = back_z(side(i))
            for e in (1, 3, 2):
                n_here(j, piece % 2, e, piece // 2).wait_recv()
                for d in (1, 3, 2):
                    f_copy(j, piece % 2, e, d, piece // 2).start()

        loop(0, 8, body)
        for axis in range(2):
            loop(1, 4, lambda d: o_all(j, axis, d, True).wait_recv())

    def cross(j):
        def body(i):
            e, d = i // 4, i % 4

            @pl.when((e > 0) & (d > 0))
            def _():
                f_all(j, 0, e, d).wait_recv()
                f_all(j, 1, d, e).wait_recv()

            x_copy(j, e, d).start()
            split(j, e, d)

        loop(0, 16, body)

    @pl.when(pump)
    def _():
        loop(1, 8, lambda d: c_copy(d).start())
        u_send(0)
        loop(0, 14, lambda i: p_copy(0, i).start())
        swap().start()

        d_copy.wait_recv()
        c_here(1, 0).wait_recv()

        def both_here(d):
            c_here(0, d).wait_recv()
            c_here(1, d).wait_recv()

        loop(1, 8, both_here)
        both = jnp.concatenate([d_v[1], d_t[...]], axis=0)
        for n in range(8):
            upper = jnp.concatenate([cz[n, 0][:, :64], cz[n, 1][:, :64]], axis=1)
            lower = jnp.concatenate([cz[n, 0][:, 64:], cz[n, 1][:, 64:]], axis=1)
            e = precise(both, jnp.concatenate([upper, lower], axis=0))
            es[2 * n] = e[:64]
            es[2 * n + 1] = e[64:]
        loop(1, 16, lambda d: e_copy(d).start())
        u_send(1)

        def relay(i):
            hand(i).wait_recv()
            p_copy(1, i).start()

        loop(0, 14, relay)

        loop(1, 16, lambda d: e_copy(d).wait_recv())
        er[0] = es[r]
        eg[r // 2] = sum(er[d] for d in range(16))
        loop(0, 8, lambda d: g_copy(d).start())

        for j in range(2):

            def take(i):
                x_copy(j, i // 4, i % 4).wait_recv()
                split(j, i // 4, i % 4)

            loop(0, 16, take)

    @pl.when(chain)
    def _():
        u_send(0)
        loop(0, 8, lambda d: c_copy(d).start())
        d_copy.start()
        swap().start()
        loop(0, 14, lambda i: hand(i).start())

        u_arrive(0)
        gx[0, x, y, z // 2, z % 2] = sum(ur[0, i] for i in range(16))
        loop(1, 8, lambda d: z_copy(0, d).start())
        u_send(1)
        spread(0)
        forward(0)

        u_arrive(1)
        total = sum(ur[1, i] for i in range(16))
        tile = [gx[0, x, 2 * (y // 2) + hh, n // 2, n % 2] for n in range(8) for hh in range(2)]
        loop(0, 8, lambda d: g_here(d).wait_recv())
        e = jnp.concatenate([eg[n] for n in range(8)], axis=1)
        gx[1, x, y, z // 2, z % 2] = total - precise(e, jnp.concatenate(tile, axis=0))
        loop(1, 8, lambda d: z_copy(1, d).start())
        spread(1)
        cross(0)
        forward(1)
        cross(1)

    for n in range(8):
        for j in range(2):
            adj_v[j, :, 128 * n : 128 * n + 128] = gx[j, n // 2, 2 * (n % 2) + k, z // 2, z % 2]
    adj_out = pltpu.make_async_copy(adj_v, adj_ref, st.at[0])
    adj_out.start()

    loads[4].wait()
    loads[5].wait()
    swap_here().wait_recv()

    def update(there):
        block = jnp.concatenate([pr_v[there, 0], pr_v[there, 1]], axis=1)
        high = block.astype(BF16)
        low = (block - high.astype(F32)).astype(BF16)
        both = jnp.concatenate([high, low], axis=0)
        for n in range(4):
            x_high = jnp.concatenate([xh[2 * n + i, there].reshape(256, 128) for i in range(2)], axis=1)
            x_low = jnp.concatenate([xl[2 * n + i, there].reshape(256, 128) for i in range(2)], axis=1)
            one, two = coarse(both, x_high), coarse(high, x_low)
            o_v[:, 256 * n : 256 * n + 256] -= one[:256] + (two + one[256:])

    def step(i):
        @pl.when(i > 0)
        def _():
            p_here(0, i - 1).wait_recv()
            p_here(1, i - 1).wait_recv()

        update(jnp.where(i == 0, z, back_z(away(i - 1))))

    loop(0, 8, step)
    out = pltpu.make_async_copy(o_v, out_ref, st.at[1])
    out.start()

    swap().wait_send()
    loop(1, 8, lambda d: c_copy(d).wait_send())
    for j in range(2):
        u_sent(j)

    @pl.when(pump)
    def _():
        def left(i):
            p_copy(0, i).wait_send()
            p_copy(1, i).wait_send()

        loop(0, 14, left)
        loop(1, 16, lambda d: e_copy(d).wait_send())
        loop(0, 8, lambda d: g_copy(d).wait_send())

    @pl.when(chain)
    def _():
        d_copy.wait_send()
        c_copy(0).wait_send()
        loop(0, 14, lambda i: hand(i).wait_send())
        for j in range(2):
            loop(1, 8, lambda d: z_copy(j, d).wait_send())
            loop(0, 16, lambda i: x_copy(j, i // 4, i % 4).wait_send())
            for axis in range(2):

                def left(e):
                    o_all(j, axis, e, False).wait_send()
                    loop(0, 4, lambda i: n_copy(j, axis, e, i, axis, True).wait_send())
                    loop(1, 4, lambda d: f_all(j, axis, e, d).wait_send())

                loop(1, 4, left)

    adj_out.wait()
    out.wait()


def body(diag_inverse, coupling, rhs_top, panel, rhs_rest):
    vmem, sem = pltpu.VMEM, pltpu.SemaphoreType.DMA
    scratch = [
        vmem((2, 64, 64), F32), vmem((64, 64), F32), vmem((2, 64, 1024), F32), vmem((16, 2, 256, 128), F32),
        vmem((8, 2, 256, 128), F32), vmem((256, 1024), F32), vmem((2, 64, 1024), F32), vmem((64, 64), F32),
        vmem((8, 2, 32, 128), F32), vmem((2, 8, 64, 128), F32), vmem((2, 16, 64, 128), F32),
        vmem((16, 64, 128), F32), vmem((16, 64, 128), F32), vmem((8, 64, 128), F32),
        vmem((2, 4, 4, 4, 2, 64, 128), F32), vmem((8, 8, 2, 2, 64, 128), BF16), vmem((8, 8, 2, 2, 64, 128), BF16),
        sem((6,)), sem((2,)), sem((2, 14)), sem((2, 7)), sem((15,)), sem((15,)), sem, sem, sem((8,)), sem((2, 8)),
        sem((2, 8)), sem((2, 16)), sem((16,)), sem((16,)), sem((8,)), sem((8,)), sem((2, 8)), sem((2, 8)),
        sem((2, 2, 4, 4)), sem((2, 2, 4, 4)), sem((2, 2, 4)), sem((2, 2, 4)), sem((2, 2, 4, 4)), sem((2, 2, 4, 4)), sem((2, 4, 4)), sem((2, 4, 4)),
    ]
    return pl.pallas_call(
        kernel,
        out_shape=(jax.ShapeDtypeStruct((2, 64, 1024), F32), jax.ShapeDtypeStruct((256, 1024), F32)),
        in_specs=[pl.BlockSpec(memory_space=pl.ANY)] * 5,
        out_specs=[pl.BlockSpec(memory_space=pl.ANY)] * 2,
        scratch_shapes=scratch,
        compiler_params=pltpu.CompilerParams(collective_id=0, has_side_effects=True, vmem_limit_bytes=60 * 2**20),
        name="window",
    )(diag_inverse, coupling, rhs_top, panel.reshape(16, 256, 128), rhs_rest)


def solution(mesh):
    in_specs = (
        P(None, "pcol", "prow"),
        P("prow", "pcol"),
        P(None, "prow", None),
        P("prow", "pcol"),
        P(("prow", "pcol"), None),
    )
    out_specs = (P(None, "pcol", None), P(("prow", "pcol"), None))
    return jax.shard_map(body, mesh=mesh, in_specs=in_specs, out_specs=out_specs, check_vma=False)
```

time: 94.2 us -> 79.4 us (0.84)
  Pallas kernels: 88.2 us -> 74.1 us
    pallas_call x1, Pallas kernels: 88.2 us -> 74.1 us  [body(): pl.pallas_call(kernel, out_shape=(jax.ShapeDtypeStruct((2, 64, 1024), F32...]
where the time goes in v3:
time: 79.4 us; the launch traced here: 78.9 us
  Pallas kernels  74.1 us (93%)
  local copies, waits for them, and re-layouts  4.19 us (5%)
    pallas_call x1, Pallas kernels, body(): pl.pallas_call(kernel, out_shape=(jax.ShapeDtypeStruct((2, 64, 1024), F32...  74.1 us
    unnamed x2, local copies, waits for them, and re-layouts  4.19 us

profile of v3, /device:TPU:1, one launch (start us, length us, event | category | flops | bytes accessed | tf_op | source)
XLA Modules:
  0.0 78.9 jit_solution(9687218098882561854)
XLA Ops:
  0.6 74.1 %window.1 = (f32[2,64,1024]{2,1,0:T(8,128)}, f32[256,1024]{1,0:T(8,128)}) custom-call(f32[2,64,64]{2,1,0:T(8,128)} %d_ref.1, f32[64,64]{1,0:T(8,128)} %c_ref.1, f32[2,64,1024]{2,1,0:T(8,128)} %b_ref.1, f32[16,256,128]{2,1,0:T(8,128)} %bitcast.1, f32[256,1024]{1,0:T(8,128)} %rest_ref.1), custom_call_target="tpu_custom_call" | custom-call | tf_op jit(solution)/shard_map/window/pallas_call | solution.py:421
  74.7 1.9 %copy.9 = f32[2,64,1024]{2,1,0:T(8,128)} copy(f32[2,64,1024]{2,1,0:T(8,128)} %get-tuple-element.4) | data formatting | bytes 1048576
  76.6 2.3 %copy.10 = f32[256,1024]{1,0:T(8,128)} copy(f32[256,1024]{1,0:T(8,128)} %get-tuple-element.5) | data formatting | bytes 2097152

commit v4 on v3

v4 whole, which is shorter than its diff:
```python
import jax
import jax.numpy as jnp
from jax import lax
from jax.experimental import pallas as pl
from jax.experimental.pallas import tpu as pltpu
from jax.sharding import PartitionSpec as P

MESH = pl.DeviceIdType.MESH
F32, BF16 = jnp.float32, jnp.bfloat16


def precise(a, b):
    return jnp.dot(a, b, precision=lax.Precision.HIGHEST, preferred_element_type=F32)


def coarse(a, b):
    return jnp.dot(a, b, preferred_element_type=F32)


def remote(src, dst, send, recv, device):
    return pltpu.make_async_remote_copy(
        src_ref=src, dst_ref=dst, send_sem=send, recv_sem=recv, device_id=device, device_id_type=MESH
    )


def loop(low, high, body):
    def step(i, carry):
        body(i)
        return carry

    lax.fori_loop(low, high, step, 0)


def kernel(
    d_ref, c_ref, b_ref, p_ref, rest_ref, adj_ref, out_ref,
    d_v, c_v, b_v, p_v, pr_v, o_v, adj_v, d_t,
    cz, us, ur, es, er, eg, gx, xh, xl,
    ld, st, p_s, p_r, h_s, h_r, w_s, w_r, d_s, d_r, c_s, c_r, u_s, u_r, e_s, e_r, g_s, g_r, z_s, z_r, n_s, n_r, o_r, f_s, f_r, x_s, x_r,
):
    r, c = lax.axis_index("prow"), lax.axis_index("pcol")
    x, y, z, k = r // 4, r % 4, c // 2, c % 2
    h = r % 2
    twin = c + 1 - 2 * k
    pump, chain = k == 0, k == 1

    def row(d):
        return (r + d) % 16

    def at_z(d):
        return (z + d) % 8

    def back_z(d):
        return (z + 8 - d) % 8

    loads = [
        pltpu.make_async_copy(src, dst, ld.at[i])
        for i, (src, dst) in enumerate(
            [(d_ref, d_v), (c_ref, c_v), (b_ref, b_v), (p_ref, p_v.at[:, 0]), (rest_ref, o_v), (p_ref.at[c], pr_v.at[z, k])]
        )
    ]
    for load in loads:
        load.start()

    barrier = pltpu.get_barrier_semaphore()

    def greet(*device):
        pl.semaphore_signal(barrier, inc=1, device_id=device, device_id_type=MESH)

    greet(r, twin)
    loop(2, 16, lambda d: greet(r, (2 * z + d) % 16))

    loop(1, 16, lambda d: greet(row(d), c))

    @pl.when(chain & (h == 0))
    def _():
        loop(1, 16, lambda d: greet(row(d), twin))

    @pl.when(chain & (h == 1))
    def _():
        loop(1, 8, lambda d: greet(row(2 * d), twin))

    for load in loads[:3]:
        load.wait()
    for j in range(2):
        u = precise(d_v[j], b_v[j])
        for n in range(8):
            us[j, n] = u[:, 128 * n : 128 * n + 128]
    cz[c] = jnp.concatenate([c_v[:32], c_v[32:]], axis=1)

    @pl.when(chain & (h == 1))
    def _():
        for j in range(2):
            pltpu.make_async_copy(us.at[j, r // 2], ur.at[j, r], u_r.at[j]).start()

    loads[3].wait()

    @pl.when(pump)
    def _():
        pl.semaphore_wait(barrier, 37 + 8 * h)

    @pl.when(chain)
    def _():
        pl.semaphore_wait(barrier, 30)

    def away(i):
        return (4 + (2 * (i % 2) - 1) * ((i + 1) // 2)) % 8

    def p_copy(kk, i):
        q = 2 * at_z(away(i // 2)) + i % 2
        return remote(p_v.at[q, kk], pr_v.at[z, kk], p_s, p_r.at[i // 2], (r, q))

    def p_here(i):
        block = pr_v.at[back_z(away(i))]
        return remote(block, block, p_s, p_r.at[i], (r, twin))

    def hand(i):
        q = 2 * at_z(away(i // 2)) + i % 2
        return remote(p_v.at[q, 0], p_v.at[q, 1], h_s, h_r, (r, twin))

    def swap():
        return remote(p_v.at[twin, 0], pr_v.at[z, k], w_s, w_r, (r, twin))

    def group(block, sem):
        return remote(block, block, sem, sem, (r, twin))

    d_copy = remote(d_v.at[1], d_t, d_s, d_r, (r, twin))

    def c_copy(d):
        return remote(cz.at[c], cz.at[c], c_s, c_r, (r, 2 * at_z(d)))

    def u_send(j):
        def body(n):
            @pl.when(pump | (2 * n + 1 != r))
            def _():
                remote(us.at[j, n], ur.at[j, r], u_s, u_r.at[j], (2 * n + k, 2 * z + 1)).start()

        loop(0, 8, body)

    def e_copy(d):
        return remote(es.at[row(d)], er.at[d], e_s, e_r, (row(d), c))

    def g_copy(d):
        return remote(eg.at[r // 2], eg.at[r // 2], g_s, g_r, (row(2 * d), 2 * z + 1))

    def z_copy(j, d):
        block = gx.at[j, x, y, z // 2, z % 2]
        return remote(block, block, z_s, z_r.at[j, d], (r, 2 * at_z(d) + k))

    def z_here(j, d):
        block = gx.at[j, x, y, back_z(d) // 2, back_z(d) % 2]
        return remote(block, block, z_s, z_r.at[j, d], (r, c))

    def along(axis, d):
        return (((x + d) % 4) * 4 + y, c) if axis == 0 else (x * 4 + (y + d) % 4, c)

    def n_copy(j, axis, d, i, a):
        block = gx.at[j, x, y, i, a]
        return remote(block, block, n_s, n_r.at[j, i, a] if axis == a else o_r.at[j], along(axis, d))

    def f_copy(j, a, e, d, i):
        block = gx.at[j, (x + 4 - (1 - a) * e) % 4, (y + 4 - a * e) % 4, i, a]
        to = ((x + a * d) % 4) * 4 + (y + (1 - a) * d) % 4
        return remote(block, block, f_s.at[j], f_r.at[j, (1 - a) * e + a * d], (to, c))

    def x_copy(j, e):
        block = gx.at[j, (x + 4 - e) % 4]
        return remote(block, block, x_s.at[j], x_r.at[j, e], (r, twin))

    def split(j, e, d):
        xx, yy = (x + 4 - e) % 4, (y + 4 - d) % 4
        p, hh = 2 * xx + yy // 2, yy % 2

        def body(i):
            value = gx[j, xx, yy, i // 2, i % 2]
            high = value.astype(BF16)
            xh[p, i, hh, j] = high
            xl[p, i, hh, j] = (value - high.astype(F32)).astype(BF16)

        loop(0, 8, body)

    def side(i):
        return ((2 * (i % 2) - 1) * ((i + 1) // 2) + 8) % 8

    def spread(j):
        def body(i):
            @pl.when(i > 0)
            def _():
                z_here(j, side(i)).wait_recv()

            piece = back_z(side(i))
            for a in range(2):

                @pl.when(piece % 2 == a)
                def _():
                    for axis in (a, 1 - a):
                        for d in (1, 3, 2):
                            n_copy(j, axis, d, piece // 2, a).start()

        loop(0, 8, body)

    def forward(j):
        def body(i):
            piece = back_z(side(i))
            n, a = piece // 2, piece % 2
            group(gx.at[j, 0:3, y, n, a], n_r.at[j, n, a]).wait_recv()
            for e in (1, 3, 2):
                for d in (1, 3, 2):
                    f_copy(j, a, e, d, n).start()

        loop(0, 8, body)
        group(gx.at[j, 0:3, 0], o_r.at[j]).wait_recv()

    def take(j, e):
        loop(0, 4, lambda d: split(j, e, d))

    def cross(j):
        for e in (0, 1, 3, 2):
            if e:
                group(gx.at[j, x, 0:3], f_r.at[j, e]).wait_recv()
            x_copy(j, e).start()
            take(j, e)

    @pl.when(pump)
    def _():
        loop(1, 8, lambda d: c_copy(d).start())
        u_send(0)
        loop(0, 14, lambda i: p_copy(0, i).start())
        swap().start()

        d_copy.wait_recv()
        group(cz.at[0:15], c_r).wait_recv()
        both = jnp.concatenate([d_v[1], d_t[...]], axis=0)
        for n in range(8):
            upper = jnp.concatenate([cz[2 * n][:, :64], cz[2 * n + 1][:, :64]], axis=1)
            lower = jnp.concatenate([cz[2 * n][:, 64:], cz[2 * n + 1][:, 64:]], axis=1)
            e = precise(both, jnp.concatenate([upper, lower], axis=0))
            es[2 * n] = e[:64]
            es[2 * n + 1] = e[64:]
        loop(1, 16, lambda d: e_copy(d).start())
        u_send(1)

        group(p_v.at[0:7], h_r).wait_recv()
        loop(0, 14, lambda i: p_copy(1, i).start())

        group(er.at[1:16], e_r).wait_recv()
        er[0] = es[r]
        eg[r // 2] = sum(er[d] for d in range(16))
        loop(0, 8, lambda d: g_copy(d).start())

        for j in range(2):
            for e in (0, 1, 3, 2):
                x_copy(j, e).wait_recv()
                take(j, e)

    @pl.when(chain)
    def _():
        u_send(0)
        loop(0, 8, lambda d: c_copy(d).start())
        d_copy.start()
        swap().start()
        loop(0, 14, lambda i: hand(i).start())

        group(ur.at[0], u_r.at[0]).wait_recv()
        gx[0, x, y, z // 2, z % 2] = sum(ur[0, i] for i in range(16))
        loop(1, 8, lambda d: z_copy(0, d).start())
        u_send(1)
        spread(0)
        forward(0)

        group(ur.at[1], u_r.at[1]).wait_recv()
        total = sum(ur[1, i] for i in range(16))
        tile = [gx[0, x, 2 * (y // 2) + hh, n // 2, n % 2] for n in range(8) for hh in range(2)]
        group(eg, g_r).wait_recv()
        e = jnp.concatenate([eg[n] for n in range(8)], axis=1)
        gx[1, x, y, z // 2, z % 2] = total - precise(e, jnp.concatenate(tile, axis=0))
        loop(1, 8, lambda d: z_copy(1, d).start())
        spread(1)
        cross(0)
        forward(1)
        cross(1)

    for n in range(8):
        for j in range(2):
            adj_v[j, :, 128 * n : 128 * n + 128] = gx[j, n // 2, 2 * (n % 2) + k, z // 2, z % 2]
    adj_out = pltpu.make_async_copy(adj_v, adj_ref, st.at[0])
    adj_out.start()

    swap().wait_send()

    @pl.when(pump)
    def _():
        group(cz.at[0:7], c_s).wait_send()
        group(us, u_s).wait_send()
        group(es.at[0:15], e_s).wait_send()
        group(eg, g_s).wait_send()

    @pl.when(chain)
    def _():
        group(cz.at[0:8], c_s).wait_send()

        @pl.when(h == 0)
        def _():
            group(us, u_s).wait_send()

        @pl.when(h == 1)
        def _():
            group(us.at[:, 0:7], u_s).wait_send()

        d_copy.wait_send()
        group(p_v.at[0:7], h_s).wait_send()
        group(er.at[0:14], z_s).wait_send()
        group(gx.at[0, 0:3], n_s).wait_send()
        for j in range(2):
            group(gx.at[j, 0:3, 0:3], f_s.at[j]).wait_send()

    loads[4].wait()
    loads[5].wait()
    swap().wait_recv()
    out = [
        pltpu.make_async_copy(o_v.at[:, 256 * n : 256 * n + 256], out_ref.at[:, 256 * n : 256 * n + 256], st.at[1])
        for n in range(4)
    ]

    def update(there, last):
        block = jnp.concatenate([pr_v[there, 0], pr_v[there, 1]], axis=1)
        high = block.astype(BF16)
        low = (block - high.astype(F32)).astype(BF16)
        both = jnp.concatenate([high, low], axis=0)
        for n in range(4):
            x_high = jnp.concatenate([xh[2 * n + i, there].reshape(256, 128) for i in range(2)], axis=1)
            x_low = jnp.concatenate([xl[2 * n + i, there].reshape(256, 128) for i in range(2)], axis=1)
            one, two = coarse(both, x_high), coarse(high, x_low)
            o_v[:, 256 * n : 256 * n + 256] -= one[:256] + (two + one[256:])
            if last:
                out[n].start()

    update(z, False)

    def step(i):
        p_here(i).wait_recv()
        update(back_z(away(i)), False)

    loop(0, 6, step)
    p_here(6).wait_recv()
    update(back_z(away(6)), True)

    @pl.when(pump)
    def _():
        group(p_v.at[0:14], p_s).wait_send()

    @pl.when(chain)
    def _():
        for j in range(2):
            group(gx.at[j], x_s.at[j]).wait_send()

    adj_out.wait()
    group(o_v, st.at[1]).wait_recv()


def body(diag_inverse, coupling, rhs_top, panel, rhs_rest):
    vmem, sem = pltpu.VMEM, pltpu.SemaphoreType.DMA
    scratch = [
        vmem((2, 64, 64), F32), vmem((64, 64), F32), vmem((2, 64, 1024), F32), vmem((16, 2, 256, 128), F32),
        vmem((8, 2, 256, 128), F32), vmem((256, 1024), F32), vmem((2, 64, 1024), F32), vmem((64, 64), F32),
        vmem((16, 32, 128), F32), vmem((2, 8, 64, 128), F32), vmem((2, 16, 64, 128), F32),
        vmem((16, 64, 128), F32), vmem((16, 64, 128), F32), vmem((8, 64, 128), F32),
        vmem((2, 4, 4, 4, 2, 64, 128), F32), vmem((8, 8, 2, 2, 64, 128), BF16), vmem((8, 8, 2, 2, 64, 128), BF16),
        sem((6,)), sem((2,)), sem, sem((7,)), sem, sem, sem, sem, sem, sem, sem, sem,
        sem, sem((2,)), sem, sem, sem, sem, sem, sem((2, 8)),
        sem, sem((2, 4, 2)), sem((2,)), sem((2,)), sem((2, 4)), sem((2,)), sem((2, 4)),
    ]
    return pl.pallas_call(
        kernel,
        out_shape=(jax.ShapeDtypeStruct((2, 64, 1024), F32), jax.ShapeDtypeStruct((256, 1024), F32)),
        in_specs=[pl.BlockSpec(memory_space=pl.ANY)] * 5,
        out_specs=[pl.BlockSpec(memory_space=pl.ANY)] * 2,
        scratch_shapes=scratch,
        compiler_params=pltpu.CompilerParams(collective_id=0, has_side_effects=True, vmem_limit_bytes=60 * 2**20),
        name="window",
    )(diag_inverse, coupling, rhs_top, panel.reshape(16, 256, 128), rhs_rest)


def solution(mesh):
    in_specs = (
        P(None, "pcol", "prow"),
        P("prow", "pcol"),
        P(None, "prow", None),
        P("prow", "pcol"),
        P(("prow", "pcol"), None),
    )
    out_specs = (P(None, "pcol", None), P(("prow", "pcol"), None))
    return jax.shard_map(body, mesh=mesh, in_specs=in_specs, out_specs=out_specs, check_vma=False)
```

time: 79.4 us -> 74.7 us (0.941)
  Pallas kernels: 74.1 us -> 68.9 us
    pallas_call x1, Pallas kernels: 74.1 us -> 68.9 us  [body(): pl.pallas_call(kernel, out_shape=(jax.ShapeDtypeStruct((2, 64, 1024), F32...]
where the time goes in v4:
time: 74.7 us; the launch traced here: 73.8 us
  Pallas kernels  68.9 us (92%)
  local copies, waits for them, and re-layouts  4.19 us (6%)
    pallas_call x1, Pallas kernels, body(): pl.pallas_call(kernel, out_shape=(jax.ShapeDtypeStruct((2, 64, 1024), F32...  68.9 us
    unnamed x2, local copies, waits for them, and re-layouts  4.19 us

profile of v4, /device:TPU:1, one launch (start us, length us, event | category | flops | bytes accessed | tf_op | source)
XLA Modules:
  0.0 73.8 jit_solution(15575965326786972696)
XLA Ops:
  0.6 68.9 %window.1 = (f32[2,64,1024]{2,1,0:T(8,128)}, f32[256,1024]{1,0:T(8,128)}) custom-call(f32[2,64,64]{2,1,0:T(8,128)} %d_ref.1, f32[64,64]{1,0:T(8,128)} %c_ref.1, f32[2,64,1024]{2,1,0:T(8,128)} %b_ref.1, f32[16,256,128]{2,1,0:T(8,128)} %bitcast.1, f32[256,1024]{1,0:T(8,128)} %rest_ref.1), custom_call_target="tpu_custom_call" | custom-call | tf_op jit(solution)/shard_map/window/pallas_call | solution.py:372
  69.6 1.9 %copy.9 = f32[2,64,1024]{2,1,0:T(8,128)} copy(f32[2,64,1024]{2,1,0:T(8,128)} %get-tuple-element.4) | data formatting | bytes 1048576
  71.5 2.3 %copy.10 = f32[256,1024]{1,0:T(8,128)} copy(f32[256,1024]{1,0:T(8,128)} %get-tuple-element.5) | data formatting | bytes 2097152

commit v5 on v4

--- a/solution.py
+++ b/solution.py
@@ -34,8 +34,8 @@
 def kernel(
     d_ref, c_ref, b_ref, p_ref, rest_ref, adj_ref, out_ref,
     d_v, c_v, b_v, p_v, pr_v, o_v, adj_v, d_t,
-    cz, us, ur, es, er, eg, gx, xh, xl,
-    ld, st, p_s, p_r, h_s, h_r, w_s, w_r, d_s, d_r, c_s, c_r, u_s, u_r, e_s, e_r, g_s, g_r, z_s, z_r, n_s, n_r, o_r, f_s, f_r, x_s, x_r,
+    cz, us, ur, es, er, eg, gx, xh, xl, tf, th,
+    ld, st, p_s, p_r, t_r, h_s, h_r, w_s, w_r, d_s, d_r, c_s, c_r, u_s, u_r, e_s, e_r, g_s, g_r, z_s, z_r, n_s, n_r, o_r, q_r, f_s, f_r, x_s, x_r,
 ):
     r, c = lax.axis_index("prow"), lax.axis_index("pcol")
     x, y, z, k = r // 4, r % 4, c // 2, c % 2
@@ -102,20 +102,53 @@
     def _():
         pl.semaphore_wait(barrier, 30)
 
-    def away(i):
-        return (4 + (2 * (i % 2) - 1) * ((i + 1) // 2)) % 8
-
-    def p_copy(kk, i):
-        q = 2 * at_z(away(i // 2)) + i % 2
-        return remote(p_v.at[q, kk], pr_v.at[z, kk], p_s, p_r.at[i // 2], (r, q))
+    def ahead(s, d):
+        return (z + d * (1 + 6 * s)) % 8
+
+    def behind(s, d):
+        return (z + d * (7 - 6 * s)) % 8
+
+    def p_near(kk):
+        for s in range(2):
+            for i in range(2):
+                q = 2 * ahead(s, 1) + i
+                remote(p_v.at[q, kk], pr_v.at[z, kk], p_s.at[s], p_r.at[s, 1], (r, q)).start()
+
+    def p_far(s, d):
+        if d == 4:
+            block, held = p_v.at[2 * ahead(s, 4) + s], th.at[s, 0]
+        else:
+            block, held = p_v.at[pl.ds(2 * ahead(s, d), 2)], tf.at[s, 3 - d]
+        remote(block, held, p_s.at[s], t_r.at[s, 4 - d], (r, 2 * ahead(s, 1))).start()
+
+    def p_pass(s, d, n):
+        to = 2 * ahead(s, 1)
+        if d == 4:
+            held, sem = th.at[s, n - 1], t_r.at[s, (0, 3, 5)[n - 1]]
+        else:
+            held, sem = (tf.at[s, 3 - d], t_r.at[s, 4 - d]) if n == 1 else (tf.at[s, 2], t_r.at[s, 4])
+        group(held, sem).wait_recv()
+        if n < d - 1:
+            on, sem = (th.at[s, n], t_r.at[s, (3, 5)[n - 1]]) if d == 4 else (tf.at[s, 2], t_r.at[s, 4])
+            remote(held, on, p_s.at[s], sem, (r, to)).start()
+        elif d == 4:
+            remote(held, pr_v.at[behind(s, n)], p_s.at[s], p_r.at[s, 4], (r, to + s)).start()
+        else:
+            for i in range(2):
+                remote(held.at[i], pr_v.at[behind(s, n)], p_s.at[s], p_r.at[s, d], (r, to + i)).start()
+
+    def both_ways(body):
+        for s in range(2):
+            body(s)
 
     def p_here(i):
-        block = pr_v.at[back_z(away(i))]
-        return remote(block, block, p_s, p_r.at[i], (r, twin))
-
-    def hand(i):
-        q = 2 * at_z(away(i // 2)) + i % 2
-        return remote(p_v.at[q, 0], p_v.at[q, 1], h_s, h_r, (r, twin))
+        d, s = (i + 1) // 2, (i + 1) % 2
+        block = pr_v.at[back_z(side(i))]
+        return group(block, p_r.at[s, d])
+
+    def hand(n, i):
+        q = 2 * at_z((4 + (2 * (n % 2) - 1) * ((n + 1) // 2)) % 8) + i
+        return remote(p_v.at[q, 0], p_v.at[q, 1], h_s, h_r.at[(n + 1) // 4], (r, twin))
 
     def swap():
         return remote(p_v.at[twin, 0], pr_v.at[z, k], w_s, w_r, (r, twin))
@@ -146,6 +179,10 @@
         block = gx.at[j, x, y, z // 2, z % 2]
         return remote(block, block, z_s, z_r.at[j, d], (r, 2 * at_z(d) + k))
 
+    def z_pass(j, d, on):
+        block = gx.at[j, x, y, back_z(d) // 2, back_z(d) % 2]
+        return remote(block, block, z_s, z_r.at[j, (d + on) % 8], (r, 2 * at_z(on) + k))
+
     def z_here(j, d):
         block = gx.at[j, x, y, back_z(d) // 2, back_z(d) % 2]
         return remote(block, block, z_s, z_r.at[j, d], (r, c))
@@ -155,16 +192,18 @@
 
     def n_copy(j, axis, d, i, a):
         block = gx.at[j, x, y, i, a]
-        return remote(block, block, n_s, n_r.at[j, i, a] if axis == a else o_r.at[j], along(axis, d))
-
-    def f_copy(j, a, e, d, i):
-        block = gx.at[j, (x + 4 - (1 - a) * e) % 4, (y + 4 - a * e) % 4, i, a]
-        to = ((x + a * d) % 4) * 4 + (y + (1 - a) * d) % 4
-        return remote(block, block, f_s.at[j], f_r.at[j, (1 - a) * e + a * d], (to, c))
-
-    def x_copy(j, e):
-        block = gx.at[j, (x + 4 - e) % 4]
-        return remote(block, block, x_s.at[j], x_r.at[j, e], (r, twin))
+        sem = n_r.at[j, i, a] if axis == a else q_r.at[j, i, a] if d == 2 else o_r.at[j]
+        return remote(block, block, n_s, sem, along(axis, d))
+
+    def f_copy(j, i, a, dx, dy, mx, my):
+        block = gx.at[j, (x + 4 - dx) % 4, (y + 4 - dy) % 4, i, a]
+        across, down = (dx + mx) % 4, (dy + my) % 4
+        sem = f_r.at[j, jnp.where(across == 2, 4 + down, across)]
+        return remote(block, block, f_s.at[j], sem, (((x + mx) % 4) * 4 + (y + my) % 4, c))
+
+    def x_copy(j, e, d=None):
+        block = gx.at[j, (x + 4 - e) % 4] if d is None else gx.at[j, (x + 4 - e) % 4, (y + 4 - d) % 4]
+        return remote(block, block, x_s.at[j], x_r.at[j, e if d is None else 4 + d], (r, twin))
 
     def split(j, e, d):
         xx, yy = (x + 4 - e) % 4, (y + 4 - d) % 4
@@ -181,13 +220,37 @@
     def side(i):
         return ((2 * (i % 2) - 1) * ((i + 1) // 2) + 8) % 8
 
+    def z_send(j):
+        for d in (2, 6, 1, 7):
+            z_copy(j, d).start()
+
+    def turn(i):
+        pair = (i + 1) // 2
+        return side(i + jnp.where(pair == 1, 2, jnp.where(pair == 2, -2, 0)))
+
     def spread(j):
         def body(i):
             @pl.when(i > 0)
             def _():
-                z_here(j, side(i)).wait_recv()
-
-            piece = back_z(side(i))
+                z_here(j, turn(i)).wait_recv()
+
+            @pl.when(i == 1)
+            def _():
+                z_pass(j, 2, 1).start()
+
+                @pl.when(back_z(2) % 2 == 0)
+                def _():
+                    z_pass(j, 2, 2).start()
+
+            @pl.when(i == 2)
+            def _():
+                z_pass(j, 6, 7).start()
+
+                @pl.when(back_z(6) % 2 == 1)
+                def _():
+                    z_pass(j, 6, 6).start()
+
+            piece = back_z(turn(i))
             for a in range(2):
 
                 @pl.when(piece % 2 == a)
@@ -200,32 +263,47 @@
 
     def forward(j):
         def body(i):
-            piece = back_z(side(i))
+            piece = back_z(turn(i))
             n, a = piece // 2, piece % 2
             group(gx.at[j, 0:3, y, n, a], n_r.at[j, n, a]).wait_recv()
-            for e in (1, 3, 2):
-                for d in (1, 3, 2):
-                    f_copy(j, a, e, d, n).start()
+            b = 1 - a
+            for e, goals in ((1, (1, 3)), (3, (1, 3)), (2, (1, 3, 2))):
+                for d in goals:
+                    f_copy(j, n, a, b * e, a * e, a * d, b * d).start()
+            group(gx.at[j, x, y, n, a], q_r.at[j, n, a]).wait_recv()
+            for d in (1, 3):
+                f_copy(j, n, a, 2 * a, 2 * b, b * d, a * d).start()
 
         loop(0, 8, body)
-        group(gx.at[j, 0:3, 0], o_r.at[j]).wait_recv()
+        group(gx.at[j, 0:2, 0], o_r.at[j]).wait_recv()
 
     def take(j, e):
         loop(0, 4, lambda d: split(j, e, d))
 
     def cross(j):
-        for e in (0, 1, 3, 2):
+        for e in (0, 1, 3):
             if e:
                 group(gx.at[j, x, 0:3], f_r.at[j, e]).wait_recv()
             x_copy(j, e).start()
             take(j, e)
+        for d in (0, 1, 3, 2):
+            if d:
+                group(gx.at[j, x, y], f_r.at[j, 4 + d]).wait_recv()
+            x_copy(j, 2, d).start()
+            split(j, 2, d)
 
     @pl.when(pump)
     def _():
         loop(1, 8, lambda d: c_copy(d).start())
         u_send(0)
-        loop(0, 14, lambda i: p_copy(0, i).start())
+        p_near(0)
         swap().start()
+        group(p_v.at[0:3], h_r.at[0]).wait_recv()
+        both_ways(lambda s: p_far(s, 4))
+        both_ways(lambda s: p_far(s, 3))
+        group(p_v.at[0:4], h_r.at[1]).wait_recv()
+        both_ways(lambda s: p_far(s, 2))
+        p_near(1)
 
         d_copy.wait_recv()
         group(cz.at[0:15], c_r).wait_recv()
@@ -239,18 +317,25 @@
         loop(1, 16, lambda d: e_copy(d).start())
         u_send(1)
 
-        group(p_v.at[0:7], h_r).wait_recv()
-        loop(0, 14, lambda i: p_copy(1, i).start())
+        both_ways(lambda s: p_pass(s, 4, 1))
 
         group(er.at[1:16], e_r).wait_recv()
         er[0] = es[r]
         eg[r // 2] = sum(er[d] for d in range(16))
         loop(0, 8, lambda d: g_copy(d).start())
+        both_ways(lambda s: p_pass(s, 3, 1))
+        both_ways(lambda s: p_pass(s, 2, 1))
+        both_ways(lambda s: p_pass(s, 4, 2))
+        both_ways(lambda s: p_pass(s, 3, 2))
+        both_ways(lambda s: p_pass(s, 4, 3))
 
         for j in range(2):
-            for e in (0, 1, 3, 2):
+            for e in (0, 1, 3):
                 x_copy(j, e).wait_recv()
                 take(j, e)
+            for d in (0, 1, 3, 2):
+                x_copy(j, 2, d).wait_recv()
+                split(j, 2, d)
 
     @pl.when(chain)
     def _():
@@ -258,11 +343,11 @@
         loop(0, 8, lambda d: c_copy(d).start())
         d_copy.start()
         swap().start()
-        loop(0, 14, lambda i: hand(i).start())
+        loop(0, 14, lambda i: hand(i // 2, i % 2).start())
 
         group(ur.at[0], u_r.at[0]).wait_recv()
         gx[0, x, y, z // 2, z % 2] = sum(ur[0, i] for i in range(16))
-        loop(1, 8, lambda d: z_copy(0, d).start())
+        z_send(0)
         u_send(1)
         spread(0)
         forward(0)
@@ -273,7 +358,7 @@
         group(eg, g_r).wait_recv()
         e = jnp.concatenate([eg[n] for n in range(8)], axis=1)
         gx[1, x, y, z // 2, z % 2] = total - precise(e, jnp.concatenate(tile, axis=0))
-        loop(1, 8, lambda d: z_copy(1, d).start())
+        z_send(1)
         spread(1)
         cross(0)
         forward(1)
@@ -338,15 +423,16 @@
 
     def step(i):
         p_here(i).wait_recv()
-        update(back_z(away(i)), False)
-
-    loop(0, 6, step)
-    p_here(6).wait_recv()
-    update(back_z(away(6)), True)
+        update(back_z(side(i)), False)
+
+    loop(1, 7, step)
+    group(pr_v.at[back_z(4)], p_r.at[k, 4]).wait_recv()
+    update(back_z(4), True)
 
     @pl.when(pump)
     def _():
-        group(p_v.at[0:14], p_s).wait_send()
+        for s in range(2):
+            group(gx.at[0], p_s.at[s]).wait_send()
 
     @pl.when(chain)
     def _():
@@ -365,9 +451,10 @@
         vmem((16, 32, 128), F32), vmem((2, 8, 64, 128), F32), vmem((2, 16, 64, 128), F32),
         vmem((16, 64, 128), F32), vmem((16, 64, 128), F32), vmem((8, 64, 128), F32),
         vmem((2, 4, 4, 4, 2, 64, 128), F32), vmem((8, 8, 2, 2, 64, 128), BF16), vmem((8, 8, 2, 2, 64, 128), BF16),
-        sem((6,)), sem((2,)), sem, sem((7,)), sem, sem, sem, sem, sem, sem, sem, sem,
+        vmem((2, 3, 2, 2, 256, 128), F32), vmem((2, 3, 2, 256, 128), F32),
+        sem((6,)), sem((2,)), sem((2,)), sem((2, 5)), sem((2, 6)), sem, sem((2,)), sem, sem, sem, sem, sem, sem,
         sem, sem((2,)), sem, sem, sem, sem, sem, sem((2, 8)),
-        sem, sem((2, 4, 2)), sem((2,)), sem((2,)), sem((2, 4)), sem((2,)), sem((2, 4)),
+        sem, sem((2, 4, 2)), sem((2,)), sem((2, 4, 2)), sem((2,)), sem((2, 8)), sem((2,)), sem((2, 8)),
     ]
     return pl.pallas_call(
         kernel,

time: 74.7 us -> 70.9 us (0.949)
  Pallas kernels: 68.9 us -> 65.6 us
    pallas_call x1, Pallas kernels: 68.9 us -> 65.6 us  [body(): pl.pallas_call(kernel, out_shape=(jax.ShapeDtypeStruct((2, 64, 1024), F32...]
where the time goes in v5:
time: 70.9 us; the launch traced here: 70.5 us
  Pallas kernels  65.6 us (93%)
  local copies, waits for them, and re-layouts  4.19 us (6%)
    pallas_call x1, Pallas kernels, body(): pl.pallas_call(kernel, out_shape=(jax.ShapeDtypeStruct((2, 64, 1024), F32...  65.6 us
    unnamed x2, local copies, waits for them, and re-layouts  4.19 us

profile of v5, /device:TPU:1, one launch (start us, length us, event | category | flops | bytes accessed | tf_op | source)
XLA Modules:
  0.0 70.5 jit_solution(4715627279421898262)
XLA Ops:
  0.6 65.6 %window.1 = (f32[2,64,1024]{2,1,0:T(8,128)}, f32[256,1024]{1,0:T(8,128)}) custom-call(f32[2,64,64]{2,1,0:T(8,128)} %d_ref.1, f32[64,64]{1,0:T(8,128)} %c_ref.1, f32[2,64,1024]{2,1,0:T(8,128)} %b_ref.1, f32[16,256,128]{2,1,0:T(8,128)} %bitcast.1, f32[256,1024]{1,0:T(8,128)} %rest_ref.1), custom_call_target="tpu_custom_call" | custom-call | tf_op jit(solution)/shard_map/window/pallas_call | solution.py:459
  66.3 1.9 %copy.9 = f32[2,64,1024]{2,1,0:T(8,128)} copy(f32[2,64,1024]{2,1,0:T(8,128)} %get-tuple-element.4) | data formatting | bytes 1048576
  68.1 2.3 %copy.10 = f32[256,1024]{1,0:T(8,128)} copy(f32[256,1024]{1,0:T(8,128)} %get-tuple-element.5) | data formatting | bytes 2097152

commit v6 on v5

--- a/solution.py
+++ b/solution.py
@@ -443,6 +443,19 @@
     group(o_v, st.at[1]).wait_recv()
 
 
+def settle(adj_ref, out_ref, adj_to, out_to, adj_v, out_v, in_s, to_s):
+    parts = [(out_ref, out_v, out_to, pl.ds(64 * i, 64), 0) for i in range(4)]
+    parts += [(adj_ref, adj_v, adj_to, pl.ds(i, 1), 1) for i in range(2)]
+    loads = [pltpu.make_async_copy(src.at[at], held.at[at], in_s.at[i]) for i, (src, held, _, at, _) in enumerate(parts)]
+    for load in loads:
+        load.start()
+    for load, (_, held, to, at, n) in zip(loads, parts):
+        load.wait()
+        pltpu.make_async_copy(held.at[at], to.at[at], to_s.at[n]).start()
+    pltpu.make_async_copy(out_v, out_to, to_s.at[0]).wait()
+    pltpu.make_async_copy(adj_v, adj_to, to_s.at[1]).wait()
+
+
 def body(diag_inverse, coupling, rhs_top, panel, rhs_rest):
     vmem, sem = pltpu.VMEM, pltpu.SemaphoreType.DMA
     scratch = [
@@ -456,15 +469,25 @@
         sem, sem((2,)), sem, sem, sem, sem, sem, sem((2, 8)),
         sem, sem((2, 4, 2)), sem((2,)), sem((2, 4, 2)), sem((2,)), sem((2, 8)), sem((2,)), sem((2, 8)),
     ]
-    return pl.pallas_call(
+    shapes = (jax.ShapeDtypeStruct((2, 64, 1024), F32), jax.ShapeDtypeStruct((256, 1024), F32))
+    results = pl.pallas_call(
         kernel,
-        out_shape=(jax.ShapeDtypeStruct((2, 64, 1024), F32), jax.ShapeDtypeStruct((256, 1024), F32)),
+        out_shape=shapes,
         in_specs=[pl.BlockSpec(memory_space=pl.ANY)] * 5,
         out_specs=[pl.BlockSpec(memory_space=pl.ANY)] * 2,
         scratch_shapes=scratch,
         compiler_params=pltpu.CompilerParams(collective_id=0, has_side_effects=True, vmem_limit_bytes=60 * 2**20),
         name="window",
     )(diag_inverse, coupling, rhs_top, panel.reshape(16, 256, 128), rhs_rest)
+    return pl.pallas_call(
+        settle,
+        out_shape=shapes,
+        in_specs=[pl.BlockSpec(memory_space=pl.ANY)] * 2,
+        out_specs=[pl.BlockSpec(memory_space=pl.ANY)] * 2,
+        scratch_shapes=[vmem((2, 64, 1024), F32), vmem((256, 1024), F32), sem((6,)), sem((2,))],
+        compiler_params=pltpu.CompilerParams(vmem_limit_bytes=60 * 2**20),
+        name="settle",
+    )(*results)
 
 
 def solution(mesh):

time: 70.9 us -> 68.8 us (0.970)
  local copies, waits for them, and re-layouts: 4.19 us -> 0 us
  Pallas kernels: 65.6 us -> 67.8 us
    unnamed x2 -> x0, local copies, waits for them, and re-layouts: 4.19 us -> none
    pallas_call x1 -> x2, Pallas kernels: 65.6 us -> 67.8 us  [the longest x1 65.6 us: body(): pl.pallas_call(kernel, out_shape=shapes, in_specs=[pl.BlockSpec(memory_sp...]
where the time goes in v6:
time: 68.8 us; the launch traced here: 68.4 us
  Pallas kernels  67.8 us (99%)
    pallas_call x1, Pallas kernels, body(): pl.pallas_call(kernel, out_shape=shapes, in_specs=[pl.BlockSpec(memory_sp...  65.6 us
    pallas_call x1, Pallas kernels, body(): pl.pallas_call(settle, out_shape=shapes, in_specs=[pl.BlockSpec(memory_sp...  2.15 us

profile of v6, /device:TPU:1, one launch (start us, length us, event | category | flops | bytes accessed | tf_op | source)
XLA Modules:
  0.0 68.4 jit_solution(3995756158338836347)
XLA Ops:
  0.6 65.6 %window.1 = (f32[2,64,1024]{2,1,0:T(8,128)}, f32[256,1024]{1,0:T(8,128)}) custom-call(f32[2,64,64]{2,1,0:T(8,128)} %d_ref.1, f32[64,64]{1,0:T(8,128)} %c_ref.1, f32[2,64,1024]{2,1,0:T(8,128)} %b_ref.1, f32[16,256,128]{2,1,0:T(8,128)} %bitcast.1, f32[256,1024]{1,0:T(8,128)} %rest_ref.1), custom_call_target="tpu_custom_call" | custom-call | tf_op jit(solution)/shard_map/window/pallas_call | solution.py:473
  66.3 2.2 %settle.1 = (f32[2,64,1024]{2,1,0:T(8,128)}, f32[256,1024]{1,0:T(8,128)}) custom-call(f32[2,64,1024]{2,1,0:T(8,128)} %get-tuple-element.4.adj_ref, f32[256,1024]{1,0:T(8,128)} %get-tuple-element.5.out_ref), custom_call_target="tpu_custom_call" | custom-call | tf_op jit(solution)/shard_map/settle/pallas_call | solution.py:482

commit v7 on v6

--- a/solution.py
+++ b/solution.py
@@ -35,7 +35,7 @@
     d_ref, c_ref, b_ref, p_ref, rest_ref, adj_ref, out_ref,
     d_v, c_v, b_v, p_v, pr_v, o_v, adj_v, d_t,
     cz, us, ur, es, er, eg, gx, xh, xl, tf, th,
-    ld, st, p_s, p_r, t_r, h_s, h_r, w_s, w_r, d_s, d_r, c_s, c_r, u_s, u_r, e_s, e_r, g_s, g_r, z_s, z_r, n_s, n_r, o_r, q_r, f_s, f_r, x_s, x_r,
+    ld, st, p_s, p_r, t_r, h_s, h_r, w_s, w_r, d_s, d_r, c_s, c_r, u_s, u_r, e_s, e_r, g_s, g_r, z_s, z_r, n_s, n_r, o_r, f_s, f_r, x_s, x_r,
 ):
     r, c = lax.axis_index("prow"), lax.axis_index("pcol")
     x, y, z, k = r // 4, r % 4, c // 2, c % 2
@@ -79,20 +79,25 @@
     def _():
         loop(1, 8, lambda d: greet(row(2 * d), twin))
 
-    for load in loads[:3]:
+    def partial():
+        loads[2].wait()
+        for j in range(2):
+            u = precise(d_v[j], b_v[j])
+            for n in range(8):
+                us[j, n] = u[:, 128 * n : 128 * n + 128]
+
+    for load in loads[:2]:
         load.wait()
-    for j in range(2):
-        u = precise(d_v[j], b_v[j])
-        for n in range(8):
-            us[j, n] = u[:, 128 * n : 128 * n + 128]
     cz[c] = jnp.concatenate([c_v[:32], c_v[32:]], axis=1)
+
+    @pl.when(chain)
+    def _():
+        partial()
 
     @pl.when(chain & (h == 1))
     def _():
         for j in range(2):
             pltpu.make_async_copy(us.at[j, r // 2], ur.at[j, r], u_r.at[j]).start()
-
-    loads[3].wait()
 
     @pl.when(pump)
     def _():
@@ -112,13 +117,13 @@
         for s in range(2):
             for i in range(2):
                 q = 2 * ahead(s, 1) + i
-                remote(p_v.at[q, kk], pr_v.at[z, kk], p_s.at[s], p_r.at[s, 1], (r, q)).start()
-
-    def p_far(s, d):
-        if d == 4:
-            block, held = p_v.at[2 * ahead(s, 4) + s], th.at[s, 0]
-        else:
-            block, held = p_v.at[pl.ds(2 * ahead(s, d), 2)], tf.at[s, 3 - d]
+                block = p_v.at[q, 1] if kk else p_ref.at[q]
+                remote(block, pr_v.at[z, kk], p_s.at[s], p_r.at[s, 1], (r, q)).start()
+
+    def p_far(s, d, kk):
+        goal = 2 * ahead(s, 4) + s if d == 4 else pl.ds(2 * ahead(s, d), 2)
+        block = p_v.at[goal, 1] if kk else p_ref.at[goal]
+        held = th.at[s, 0, kk] if d == 4 else tf.at[s, 3 - d, :, kk]
         remote(block, held, p_s.at[s], t_r.at[s, 4 - d], (r, 2 * ahead(s, 1))).start()
 
     def p_pass(s, d, n):
@@ -192,18 +197,18 @@
 
     def n_copy(j, axis, d, i, a):
         block = gx.at[j, x, y, i, a]
-        sem = n_r.at[j, i, a] if axis == a else q_r.at[j, i, a] if d == 2 else o_r.at[j]
+        sem = n_r.at[j, i, a] if axis == a or d == 2 else o_r.at[j]
         return remote(block, block, n_s, sem, along(axis, d))
 
     def f_copy(j, i, a, dx, dy, mx, my):
         block = gx.at[j, (x + 4 - dx) % 4, (y + 4 - dy) % 4, i, a]
         across, down = (dx + mx) % 4, (dy + my) % 4
-        sem = f_r.at[j, jnp.where(across == 2, 4 + down, across)]
+        sem = f_r.at[j, jnp.where(across == 2, 1 + down, (across - 1) // 2)]
         return remote(block, block, f_s.at[j], sem, (((x + mx) % 4) * 4 + (y + my) % 4, c))
 
     def x_copy(j, e, d=None):
         block = gx.at[j, (x + 4 - e) % 4] if d is None else gx.at[j, (x + 4 - e) % 4, (y + 4 - d) % 4]
-        return remote(block, block, x_s.at[j], x_r.at[j, e if d is None else 4 + d], (r, twin))
+        return remote(block, block, x_s.at[j], x_r.at[j, (e + 1) // 2 if d is None else 3 + d], (r, twin))
 
     def split(j, e, d):
         xx, yy = (x + 4 - e) % 4, (y + 4 - d) % 4
@@ -256,7 +261,7 @@
                 @pl.when(piece % 2 == a)
                 def _():
                     for axis in (a, 1 - a):
-                        for d in (1, 3, 2):
+                        for d in (1, 3, 2) if axis == a else (2, 1, 3):
                             n_copy(j, axis, d, piece // 2, a).start()
 
         loop(0, 8, body)
@@ -265,12 +270,11 @@
         def body(i):
             piece = back_z(turn(i))
             n, a = piece // 2, piece % 2
-            group(gx.at[j, 0:3, y, n, a], n_r.at[j, n, a]).wait_recv()
+            group(gx.at[j, :, y, n, a], n_r.at[j, n, a]).wait_recv()
             b = 1 - a
             for e, goals in ((1, (1, 3)), (3, (1, 3)), (2, (1, 3, 2))):
                 for d in goals:
                     f_copy(j, n, a, b * e, a * e, a * d, b * d).start()
-            group(gx.at[j, x, y, n, a], q_r.at[j, n, a]).wait_recv()
             for d in (1, 3):
                 f_copy(j, n, a, 2 * a, 2 * b, b * d, a * d).start()
 
@@ -283,26 +287,31 @@
     def cross(j):
         for e in (0, 1, 3):
             if e:
-                group(gx.at[j, x, 0:3], f_r.at[j, e]).wait_recv()
+                group(gx.at[j, x, 0:3], f_r.at[j, (e - 1) // 2]).wait_recv()
             x_copy(j, e).start()
             take(j, e)
         for d in (0, 1, 3, 2):
             if d:
-                group(gx.at[j, x, y], f_r.at[j, 4 + d]).wait_recv()
+                group(gx.at[j, x, y], f_r.at[j, 1 + d]).wait_recv()
             x_copy(j, 2, d).start()
             split(j, 2, d)
 
     @pl.when(pump)
     def _():
         loop(1, 8, lambda d: c_copy(d).start())
+        p_near(0)
+        both_ways(lambda s: p_far(s, 4, 0))
+        both_ways(lambda s: p_far(s, 3, 0))
+        partial()
         u_send(0)
-        p_near(0)
+        loads[3].wait()
         swap().start()
         group(p_v.at[0:3], h_r.at[0]).wait_recv()
-        both_ways(lambda s: p_far(s, 4))
-        both_ways(lambda s: p_far(s, 3))
+        both_ways(lambda s: p_far(s, 4, 1))
+        both_ways(lambda s: p_far(s, 3, 1))
+        both_ways(lambda s: p_far(s, 2, 0))
         group(p_v.at[0:4], h_r.at[1]).wait_recv()
-        both_ways(lambda s: p_far(s, 2))
+        both_ways(lambda s: p_far(s, 2, 1))
         p_near(1)
 
         d_copy.wait_recv()
@@ -342,6 +351,7 @@
         u_send(0)
         loop(0, 8, lambda d: c_copy(d).start())
         d_copy.start()
+        loads[3].wait()
         swap().start()
         loop(0, 14, lambda i: hand(i // 2, i % 2).start())
 
@@ -467,7 +477,7 @@
         vmem((2, 3, 2, 2, 256, 128), F32), vmem((2, 3, 2, 256, 128), F32),
         sem((6,)), sem((2,)), sem((2,)), sem((2, 5)), sem((2, 6)), sem, sem((2,)), sem, sem, sem, sem, sem, sem,
         sem, sem((2,)), sem, sem, sem, sem, sem, sem((2, 8)),
-        sem, sem((2, 4, 2)), sem((2,)), sem((2, 4, 2)), sem((2,)), sem((2, 8)), sem((2,)), sem((2, 8)),
+        sem, sem((2, 4, 2)), sem((2,)), sem((2,)), sem((2, 5)), sem((2,)), sem((2, 7)),
     ]
     shapes = (jax.ShapeDtypeStruct((2, 64, 1024), F32), jax.ShapeDtypeStruct((256, 1024), F32))
     results = pl.pallas_call(

time: 68.8 us -> 68.6 us (level)
  no operation moved by 1% of the time
where the time goes in v7:
time: 68.6 us; the launch traced here: 68.2 us
  Pallas kernels  67.6 us (99%)
    pallas_call x1, Pallas kernels, body(): pl.pallas_call(kernel, out_shape=shapes, in_specs=[pl.BlockSpec(memory_sp...  65.4 us
    pallas_call x1, Pallas kernels, body(): pl.pallas_call(settle, out_shape=shapes, in_specs=[pl.BlockSpec(memory_sp...  2.15 us

profile of v7, /device:TPU:1, one launch (start us, length us, event | category | flops | bytes accessed | tf_op | source)
XLA Modules:
  0.0 68.2 jit_solution(11418600564225584302)
XLA Ops:
  0.6 65.4 %window.1 = (f32[2,64,1024]{2,1,0:T(8,128)}, f32[256,1024]{1,0:T(8,128)}) custom-call(f32[2,64,64]{2,1,0:T(8,128)} %d_ref.1, f32[64,64]{1,0:T(8,128)} %c_ref.1, f32[2,64,1024]{2,1,0:T(8,128)} %b_ref.1, f32[16,256,128]{2,1,0:T(8,128)} %bitcast.1, f32[256,1024]{1,0:T(8,128)} %rest_ref.1), custom_call_target="tpu_custom_call" | custom-call | tf_op jit(solution)/shard_map/window/pallas_call | solution.py:483
  66.0 2.2 %settle.1 = (f32[2,64,1024]{2,1,0:T(8,128)}, f32[256,1024]{1,0:T(8,128)}) custom-call(f32[2,64,1024]{2,1,0:T(8,128)} %get-tuple-element.4.adj_ref, f32[256,1024]{1,0:T(8,128)} %get-tuple-element.5.out_ref), custom_call_target="tpu_custom_call" | custom-call | tf_op jit(solution)/shard_map/settle/pallas_call | solution.py:492

commit v8 on v7

--- a/solution.py
+++ b/solution.py
@@ -454,8 +454,8 @@
 
 
 def settle(adj_ref, out_ref, adj_to, out_to, adj_v, out_v, in_s, to_s):
-    parts = [(out_ref, out_v, out_to, pl.ds(64 * i, 64), 0) for i in range(4)]
-    parts += [(adj_ref, adj_v, adj_to, pl.ds(i, 1), 1) for i in range(2)]
+    parts = [(out_ref, out_v, out_to, pl.ds(128 * i, 128), 0) for i in range(2)]
+    parts += [(adj_ref, adj_v, adj_to, pl.ds(0, 2), 1) for i in range(1)]
     loads = [pltpu.make_async_copy(src.at[at], held.at[at], in_s.at[i]) for i, (src, held, _, at, _) in enumerate(parts)]
     for load in loads:
         load.start()
@@ -494,7 +494,7 @@
         out_shape=shapes,
         in_specs=[pl.BlockSpec(memory_space=pl.ANY)] * 2,
         out_specs=[pl.BlockSpec(memory_space=pl.ANY)] * 2,
-        scratch_shapes=[vmem((2, 64, 1024), F32), vmem((256, 1024), F32), sem((6,)), sem((2,))],
+        scratch_shapes=[vmem((2, 64, 1024), F32), vmem((256, 1024), F32), sem((3,)), sem((2,))],
         compiler_params=pltpu.CompilerParams(vmem_limit_bytes=60 * 2**20),
         name="settle",
     )(*results)

time: 68.6 us -> 68.7 us (level)
  no operation moved by 1% of the time
where the time goes in v8:
time: 68.7 us; the launch traced here: 68.3 us
  Pallas kernels  67.6 us (98%)
    pallas_call x1, Pallas kernels, body(): pl.pallas_call(kernel, out_shape=shapes, in_specs=[pl.BlockSpec(memory_sp...  65.4 us
    pallas_call x1, Pallas kernels, body(): pl.pallas_call(settle, out_shape=shapes, in_specs=[pl.BlockSpec(memory_sp...  2.22 us

profile of v8, /device:TPU:1, one launch (start us, length us, event | category | flops | bytes accessed | tf_op | source)
XLA Modules:
  0.0 68.3 jit_solution(9665234637566228319)
XLA Ops:
  0.6 65.4 %window.1 = (f32[2,64,1024]{2,1,0:T(8,128)}, f32[256,1024]{1,0:T(8,128)}) custom-call(f32[2,64,64]{2,1,0:T(8,128)} %d_ref.1, f32[64,64]{1,0:T(8,128)} %c_ref.1, f32[2,64,1024]{2,1,0:T(8,128)} %b_ref.1, f32[16,256,128]{2,1,0:T(8,128)} %bitcast.1, f32[256,1024]{1,0:T(8,128)} %rest_ref.1), custom_call_target="tpu_custom_call" | custom-call | tf_op jit(solution)/shard_map/window/pallas_call | solution.py:483
  66.0 2.2 %settle.1 = (f32[2,64,1024]{2,1,0:T(8,128)}, f32[256,1024]{1,0:T(8,128)}) custom-call(f32[2,64,1024]{2,1,0:T(8,128)} %get-tuple-element.4.adj_ref, f32[256,1024]{1,0:T(8,128)} %get-tuple-element.5.out_ref), custom_call_target="tpu_custom_call" | custom-call | tf_op jit(solution)/shard_map/settle/pallas_call | solution.py:492
